TPU v7x, 256 devices: a whole 4x4x8 slice. The times are simulated.
256 devices in a mesh: row: 4 (over x), col: 32 (over z, y), depth: 2 (over core).
Axes of the slice: x: 4, y: 4, z: 8, core: 2. Of those that a mesh axis runs over, the one named last changes fastest.
Arguments:
- tokens: bfloat16 [8192, 3200], P(('depth', 'col'), 'row'), may hold values from -6 to 6
- gain: bfloat16 [3200], P('row'), may hold values from 0.099609375 to 1.8984375
- w_up: bfloat16 [3200, 6400], P('col', 'row'), may hold values from -0.10606602 to 0.10606602
- w_down: bfloat16 [6400, 3200], P('row', 'col'), may hold values from -0.1125 to 0.1125
- cotangent: bfloat16 [8192, 3200], P(('depth', 'col'), 'row'), may hold values from -11 to 11
Outputs:
- out: bfloat16 [8192, 3200], P(('depth', 'col'), 'row')
- d_tokens: bfloat16 [8192, 3200], P(('depth', 'col'), 'row')
- grad_up: float32 [3200, 6400], P('col', 'row')
- grad_down: float32 [6400, 3200], P('row', 'col')
- grad_gain: float32 [3200], P('row')
All inputs are finite; a program needn't handle non-finite values.
Results may differ from a plain program's by a relative error of at most 0.0055.
Values may be sent and summed in bfloat16 or wider, within the bound.
A program may use at most 128 MiB of HBM per device.

v0:
```python
import math

import jax
import jax.numpy as jnp
from jax import lax
from jax.sharding import PartitionSpec as P

EPS = 1e-06


def gelu_value(pre):
    return 0.5 * pre * (1.0 + lax.erf(pre / math.sqrt(2.0)))


def gelu_slope(pre):
    return 0.5 * (1.0 + lax.erf(pre / math.sqrt(2.0))) + pre * jnp.exp(
        -0.5 * pre * pre
    ) / math.sqrt(2.0 * math.pi)


def contract(left, right, left_dim, right_dim):
    return lax.dot_general(
        left, right, (((left_dim,), (right_dim,)), ((), ())), preferred_element_type=jnp.float32
    )


def on_device(tokens, gain, w_up, w_down, cotangent):
    full_x, full_gain = (
        lax.all_gather(tokens, "row", axis=1, tiled=True),
        lax.all_gather(gain, "row", axis=0, tiled=True),
    )
    full_xf = full_x.astype(jnp.float32)
    inv = lax.rsqrt(jnp.mean(full_xf * full_xf, axis=1, keepdims=True) + EPS)
    unit_full = full_xf * inv
    full_gain_f = full_gain.astype(jnp.float32)
    normed = (unit_full * full_gain_f).astype(jnp.bfloat16)
    up_panel, down_panel = (
        lax.all_gather(w_up, "col", axis=0, tiled=True),
        lax.all_gather(w_down, "col", axis=1, tiled=True),
    )
    pre = jnp.dot(normed, up_panel, preferred_element_type=jnp.float32)
    hidden = gelu_value(pre).astype(jnp.bfloat16)
    piece = down_panel
    branch_t = lax.psum_scatter(
        contract(piece, hidden, 0, 1), "row", scatter_dimension=0, tiled=True
    )
    tokens_f = tokens.astype(jnp.float32)
    out = (tokens_f + branch_t.T).astype(jnp.bfloat16)
    full_cot = lax.all_gather(cotangent, "row", axis=1, tiled=True)
    d_hidden = contract(full_cot, down_panel, 1, 1)
    d_pre = (d_hidden * gelu_slope(pre)).astype(jnp.bfloat16)
    unit_local = tokens_f * inv
    gain_local = gain.astype(jnp.float32)
    piece = up_panel
    d_normed = lax.psum_scatter(
        contract(piece, d_pre, 1, 1), "row", scatter_dimension=0, tiled=True
    ).T
    local_dot = jnp.sum(d_normed * gain_local * unit_local, axis=1, keepdims=True)
    mean_dot = lax.psum(local_dot, "row") / full_x.shape[1]
    d_unit = d_normed * gain_local
    d_tokens = (cotangent.astype(jnp.float32) + inv * (d_unit - unit_local * mean_dot)).astype(
        jnp.bfloat16
    )
    gain_term = jnp.sum(d_normed * unit_local, axis=0)
    total_tokens = tokens.shape[0] * lax.axis_size("col") * lax.axis_size("depth")
    scale = total_tokens ** (-0.5)
    group_normed, group_cot = (
        lax.all_to_all(normed, "col", split_axis=1, concat_axis=0, tiled=True),
        lax.all_to_all(full_cot, "col", split_axis=1, concat_axis=0, tiled=True),
    )
    group_pre, group_hidden = (
        lax.all_gather(d_pre, "col", axis=0, tiled=True),
        lax.all_gather(hidden, "col", axis=0, tiled=True),
    )
    up_term = contract(group_normed, group_pre, 0, 0)
    down_term = contract(group_hidden, group_cot, 0, 0)
    grad_up, grad_down = lax.psum((up_term, down_term), "depth")
    grad_gain = lax.psum(gain_term, ("col", "depth"))
    return (out, d_tokens, grad_up * scale, grad_down * scale, grad_gain * scale)


def solution(mesh):
    in_specs = (
        P(("depth", "col"), "row"),
        P("row"),
        P("col", "row"),
        P("row", "col"),
        P(("depth", "col"), "row"),
    )
    out_specs = (
        P(("depth", "col"), "row"),
        P(("depth", "col"), "row"),
        P("col", "row"),
        P("row", "col"),
        P("row"),
    )
    return jax.shard_map(
        on_device, mesh=mesh, in_specs=in_specs, out_specs=out_specs, check_vma=False
    )
```

profile of v0, /device:TPU:1, one launch (start us, length us, event | category | flops | bytes accessed | tf_op | source)
XLA Modules:
  0.0 750.7 jit_solution(18280253170555869685)
XLA Ops:
  11.5 9.4 %all-reduce = bf16[3200]{0:T(1024)(128)(2,1)S(1)} all-reduce(bf16[3200]{0:T(1024)(128)(2,1)S(1)} %dynamic-update-slice), channel_id=1, replica_groups=mesh['row'=4,'col'=32,'depth'=2] {'row'}, use_global_device_ids=true, to_apply=%add | all-reduce | flops 3200 | bytes 12800
  20.9 12.7 %all_gather.21 = bf16[128,3200]{0,1:T(8,128)(2,1)S(1)} all-gather(bf16[128,800]{0,1:T(8,128)(2,1)} %param.5), channel_id=1, replica_groups=mesh['row'=4,'col'=32,'depth'=2] {'row'}, dimensions={1}, use_global_device_ids=true | all-gather | bytes 1024000 | tf_op jit(solution)/shard_map/all_gather | solution.py:29
  34.1 11.5 %all_gather.25 = bf16[128,3200]{0,1:T(8,128)(2,1)S(1)} all-gather(bf16[128,800]{0,1:T(8,128)(2,1)} %param.9), channel_id=1, replica_groups=mesh['row'=4,'col'=32,'depth'=2] {'row'}, dimensions={1}, use_global_device_ids=true | all-gather | bytes 1024000 | tf_op jit(solution)/shard_map/all_gather | solution.py:49
  46.1 80.2 %all-gather.11.cloned.1.call-done = bf16[32,100,1600]{2,1,0:T(8,128)(2,1)} async-done(((bf16[1,100,1600]{2,1,0:T(8,128)(2,1)}), bf16[32,100,1600]{2,1,0:T(8,128)(2,1)}) %all-gather.11.cloned.1.call-update) | async-done | bytes 10240016 | tf_op jit(solution)/shard_map/all_gather | solution.py:38
  126.2 14.7 %reshape.30 = bf16[3200,1600]{1,0:T(8,128)(2,1)} reshape(bf16[32,100,1600]{2,1,0:T(8,128)(2,1)} %all-gather.11.cloned.1.call-done) | data formatting | bytes 20480000
  140.9 8.9 %multiply_convert_fusion = (bf16[128,1600]{0,1:T(8,128)(2,1)}, f32[128,1600]{0,1:T(8,128)S(1)}) fusion(bf16[128,3200]{0,1:T(8,128)(2,1)S(1)} %fusion.3, bf16[3200,1600]{1,0:T(8,128)(2,1)} %reshape.30), kind=kOutput, calls=%fused_computation.16 | convolution fusion | flops 1311744000 | bytes 12288000 | tf_op jit(solution)/shard_map/dot_general | solution.py:41
  149.8 88.3 %all-gather.13.cloned.1.call-done = bf16[32,100,1600]{2,1,0:T(8,128)(2,1)} async-done(((bf16[1,100,1600]{2,1,0:T(8,128)(2,1)}), bf16[32,100,1600]{2,1,0:T(8,128)(2,1)}) %all-gather.13.cloned.1.call-update) | async-done | bytes 10240016 | tf_op jit(solution)/shard_map/all_gather | solution.py:39
  238.1 14.7 %reshape.32 = bf16[3200,1600]{1,0:T(8,128)(2,1)} reshape(bf16[32,100,1600]{2,1,0:T(8,128)(2,1)} %all-gather.13.cloned.1.call-done) | data formatting | bytes 20480000
  252.8 9.0 %fusion = bf16[128,1600]{0,1:T(8,128)(2,1)} fusion(bf16[128,3200]{0,1:T(8,128)(2,1)S(1)} %all_gather.25, bf16[3200,1600]{1,0:T(8,128)(2,1)} %reshape.32, f32[128,1600]{0,1:T(8,128)S(1)} %get-tuple-element.27), kind=kOutput, calls=%fused_computation.3 | convolution fusion | flops 1312768000 | bytes 12288000 | tf_op jit(solution)/shard_map/dot_general | solution.py:22
  262.6 7.4 convolution_bitcast_fusion
  272.8 5.3 all-to-all-start.1
  279.2 26.6 %all-to-all-done.1 = bf16[128,32,100]{0,2,1:T(8,128)(2,1)S(1)} async-done(((bf16[128,32,100]{0,2,1:T(8,128)(2,1)}), bf16[128,32,100]{0,2,1:T(8,128)(2,1)S(1)}, u32[]{:S(2)}, u32[]{:S(2)}) %all-to-all-start.1) | async-done | bytes 819232 | tf_op jit(solution)/shard_map/all_to_all | solution.py:69
  305.8 6.5 all-to-all-start
  312.3 7.4 convolution_bitcast_fusion.1
  322.3 14.3 %all-to-all-done = bf16[128,32,100]{0,2,1:T(8,128)(2,1)S(1)} async-done(((bf16[128,32,100]{0,2,1:T(8,128)(2,1)}), bf16[128,32,100]{0,2,1:T(8,128)(2,1)S(1)}, u32[]{:S(2)}, u32[]{:S(2)}) %all-to-all-start) | async-done | bytes 819232 | tf_op jit(solution)/shard_map/all_to_all | solution.py:68
  337.1 74.0 %all-gather.7.cloned.1.call-done = bf16[4096,1600]{0,1:T(8,128)(2,1)} async-done(((bf16[128,1600]{0,1:T(8,128)(2,1)}), bf16[4096,1600]{0,1:T(8,128)(2,1)}) %all-gather.7.cloned.1.call-update) | async-done | bytes 13107216 | tf_op jit(solution)/shard_map/all_gather | solution.py:72
  411.1 9.7 %fusion.18 = f32[100,1600]{1,0:T(8,128)} fusion(bf16[4096,100]{0,1:T(8,128)(2,1)S(1)} %bitcast.59, bf16[4096,1600]{0,1:T(8,128)(2,1)} %all-gather.7.cloned.1.call-done), kind=kOutput, calls=%fused_computation.36 | convolution fusion | flops 1310720000 | bytes 14566400 | tf_op jit(solution)/shard_map/dot_general | solution.py:22
  420.8 120.2 %all-gather.9.cloned.1.call-done = bf16[4096,1600]{0,1:T(8,128)(2,1)} async-done(((bf16[128,1600]{0,1:T(8,128)(2,1)}), bf16[4096,1600]{0,1:T(8,128)(2,1)}) %all-gather.9.cloned.1.call-update) | async-done | bytes 13107216 | tf_op jit(solution)/shard_map/all_gather | solution.py:73
  541.0 9.7 %fusion.19 = f32[1600,100]{0,1:T(8,128)} fusion(bf16[4096,1600]{0,1:T(8,128)(2,1)} %all-gather.9.cloned.1.call-done, bf16[4096,100]{0,1:T(8,128)(2,1)S(1)} %bitcast.62), kind=kOutput, calls=%fused_computation.37 | convolution fusion | flops 1310720000 | bytes 14566400 | tf_op jit(solution)/shard_map/dot_general | solution.py:22
  551.1 19.9 %reduce-scatter.9.cloned.1.call-done = f32[800,128]{1,0:T(8,128)} async-done(((f32[3200,128]{1,0:T(8,128)}), f32[800,128]{1,0:T(8,128)}) %reduce-scatter.9.cloned.1.call-update) | async-done | bytes 409616
  572.2 29.7 %reduce-scatter.7.cloned.1.call-done = f32[800,128]{1,0:T(8,128)} async-done(((f32[3200,128]{1,0:T(8,128)}), f32[800,128]{1,0:T(8,128)}) %reduce-scatter.7.cloned.1.call-update) | async-done | bytes 409616
  603.3 7.1 psum.28
  612.3 127.0 %psum.31 = f32[800]{0:T(1024)S(1)} all-reduce(f32[800]{0:T(1024)S(1)} %get-tuple-element.20), channel_id=1, replica_groups=mesh['row'=4,'col'=32,'depth'=2] {'col','depth'}, use_global_device_ids=true, to_apply=%region_8.0 | all-reduce | flops 800 | bytes 6400 | tf_op jit(solution)/shard_map/psum | solution.py:78
  739.8 2.0 broadcast_multiply_fusion.1
  (50 shorter events, 19.8 us)
Async XLA Ops:
  7.2 119.1 %all-gather.11.cloned.1.call-start = ((), (), s32[]{:S(2)}) async-start(), calls=%async_computation.6 | async-start | bytes 11421696 | tf_op jit(solution)/shard_map/all_gather | solution.py:38
  7.9 230.2 %all-gather.13.cloned.1.call-start = ((), (), s32[]{:S(2)}) async-start(), calls=%async_computation.7 | async-start | bytes 11421696 | tf_op jit(solution)/shard_map/all_gather | solution.py:39
  8.6 402.4 %all-gather.7.cloned.1.call-start = ((), (), s32[]{:S(2)}) async-start(), calls=%async_computation.4 | async-start | bytes 13516800 | tf_op jit(solution)/shard_map/all_gather | solution.py:72
  261.8 279.2 %all-gather.9.cloned.1.call-start = ((), (), s32[]{:S(2)}) async-start(), calls=%async_computation.5 | async-start | bytes 13516800 | tf_op jit(solution)/shard_map/all_gather | solution.py:73
  262.4 308.6 %reduce-scatter.9.cloned.1.call-start = ((), (), s32[]{:S(2)}) async-start(), calls=%async_computation.9 | async-start | bytes 2048000
  272.8 33.0 %all-to-all-start.1 = ((bf16[128,32,100]{0,2,1:T(8,128)(2,1)}), bf16[128,32,100]{0,2,1:T(8,128)(2,1)S(1)}, u32[]{:S(2)}, u32[]{:S(2)}) async-start(bf16[128,32,100]{0,2,1:T(8,128)(2,1)} %all_to_all.32), calls=%async_computation.1 | async-start | bytes 1703936 | tf_op jit(solution)/shard_map/all_to_all | solution.py:69
  305.8 30.8 %all-to-all-start = ((bf16[128,32,100]{0,2,1:T(8,128)(2,1)}), bf16[128,32,100]{0,2,1:T(8,128)(2,1)S(1)}, u32[]{:S(2)}, u32[]{:S(2)}) async-start(bf16[128,32,100]{0,2,1:T(8,128)(2,1)} %all_to_all.28), calls=%async_computation | async-start | bytes 1703936 | tf_op jit(solution)/shard_map/all_to_all | solution.py:68
  312.3 289.6 %reduce-scatter.7.cloned.1.call-start = ((), (), s32[]{:S(2)}) async-start(), calls=%async_computation.8 | async-start | bytes 2048000
  321.5 418.4 %all-reduce.4.cloned.1.call-start = ((), (), s32[]{:S(2)}) async-start(), calls=%async_computation.10 | async-start | bytes 2768896 | tf_op jit(solution)/shard_map/psum | solution.py:77
  420.8 129.9 %copy-start.2 = (bf16[800]{0:T(1024)(128)(2,1)S(1)}, bf16[800]{0:T(1024)(128)(2,1)}, u32[]{:S(2)}) copy-start(bf16[800]{0:T(1024)(128)(2,1)} %param.6) | copy-start | bytes 4804
  420.8 129.9 %copy-start = (bf16[128,800]{0,1:T(8,128)(2,1)S(1)}, bf16[128,800]{0,1:T(8,128)(2,1)}, u32[]{:S(2)}) copy-start(bf16[128,800]{0,1:T(8,128)(2,1)} %param.5) | copy-start | bytes 614404
  420.8 130.1 %copy-start.1 = (bf16[128,800]{0,1:T(8,128)(2,1)S(1)}, bf16[128,800]{0,1:T(8,128)(2,1)}, u32[]{:S(2)}) copy-start(bf16[128,800]{0,1:T(8,128)(2,1)} %param.9) | copy-start | bytes 614404
Sparse Core Ops, SparseCore 0:
  10.6 115.5 all-gather.10
  128.8 109.2 all-gather.12
  261.9 149.1 all-gather.6
  414.0 126.9 all-gather.8
  543.4 27.5 reduce-scatter.8
  573.5 28.2 reduce-scatter.6
  605.1 31.7 all-reduce.3
where the time goes:
time: 752 us; the launch traced here: 751 us
  waiting for transfers between devices  455 us (61%)
  blocking collectives  168 us (22%)
  matrix products  52 us (7%)
  local copies, waits for them, and re-layouts  42.5 us (6%)
  between operations  14.9 us (2%)
  starting transfers between devices  12.5 us (2%)
    psum x1, blocking collectives, on_device(): grad_gain = lax.psum(gain_term, ('col', 'depth'))  127 us
    all_gather x1, waiting for transfers between devices, on_device(): lax.all_gather(hidden, 'col', axis=0, tiled=True)  120 us
    all_gather x1, waiting for transfers between devices, on_device(): lax.all_gather(w_down, 'col', axis=1, tiled=True)  88.3 us
    all_gather x1, waiting for transfers between devices, on_device(): lax.all_gather(w_up, 'col', axis=0, tiled=True)  80.2 us
    all_gather x1, waiting for transfers between devices, on_device(): lax.all_gather(d_pre, 'col', axis=0, tiled=True)  74 us
    unnamed x9, waiting for transfers between devices  51.5 us
    dot_general x5, matrix products, contract(): lax.dot_general(left, right, (((left_dim,), (right_dim,)), ((), ())), pre...  43.1 us
    unnamed x23, local copies, waits for them, and re-layouts  40.2 us
  transfers between devices with their start and end apart: 9, of which 8 were waited for; matrix products, arithmetic and copies ran while one was open for 9% of the time, Pallas kernels for 0%

commit v1 on v0

v1 whole, which is shorter than its diff:
```python
import math

import jax
import jax.numpy as jnp
from jax import lax
from jax.experimental import pallas as pl
from jax.experimental.pallas import tpu as pltpu
from jax.sharding import PartitionSpec as P

EPS = 1e-06
MESH = pl.DeviceIdType.MESH
F32, BF16 = jnp.float32, jnp.bfloat16

NX, NY, NZ = 4, 4, 8
D, FF, TOK = 3200, 6400, 8192
DX = D // NX
TB = 128
T = NY * TB
DZ = D // NZ
DC = D // (NY * NZ)
FS = FF // (NX * NY)
FP = 512
RP = 112
EX = 16
DE = DX + EX
SUBS = ((0, 208), (208, 192))
HALF = ((0, 400), (400, 400))
HALFE = ((0, 400), (400, 416))
ORDER = (2, 1, -1, 0)
ZORDER = (4, 3, -3, 2, -2, 1, -1, 0)


def gelu_value(pre):
    return 0.5 * pre * (1.0 + lax.erf(pre / math.sqrt(2.0)))


def gelu_slope(pre):
    return 0.5 * (1.0 + lax.erf(pre / math.sqrt(2.0))) + pre * jnp.exp(
        -0.5 * pre * pre
    ) / math.sqrt(2.0 * math.pi)


def dot(left, right, left_dim, right_dim):
    return lax.dot_general(
        left, right, (((left_dim,), (right_dim,)), ((), ())), preferred_element_type=F32
    )


class Messages:
    def __init__(self, send, recv):
        self.send, self.recv, self.n, self.live = send, recv, 0, []

    def start(self, src, dst, device):
        i = self.n
        self.n += 1
        cp = pltpu.make_async_remote_copy(
            src_ref=src, dst_ref=dst, send_sem=self.send.at[i], recv_sem=self.recv.at[i],
            device_id=device, device_id_type=MESH,
        )
        cp.start()
        self.live.append(cp)
        return cp

    def drain(self):
        for cp in self.live:
            cp.wait_send()
        self.live = []


N_MESSAGES = 176


def kernel(
    x_in, c_in, w_in, g_in,
    out_ref, dtok_ref, gw_ref, gg_ref,
    xt, nc, w, wa, gr, gcol, inv_s, pre_s, dh_s, hd, md_s, g, xr, zs, zr,
    br, dn, b0, b1, bq0, bq1, d0, d1, dq0, dq1, stage, ga,
    send_sem, recv_sem, copy_sem,
):
    x = lax.axis_index("row")
    col = lax.axis_index("col")
    d = lax.axis_index("depth")
    y, z = lax.rem(col, NY), col // NY
    e = 1 - d

    def dev(ax=None, off=0):
        xx, yy, zz, dd = x, y, z, d
        if ax == "x":
            xx = lax.rem(x + (off + NX), NX)
        elif ax == "y":
            yy = lax.rem(y + (off + NY), NY)
        elif ax == "z":
            zz = lax.rem(z + (off + NZ), NZ)
        elif ax == "c":
            dd = e
        return (xx, zz * NY + yy, dd)

    def px(off):
        return lax.rem(x + (off + NX), NX)

    def py(off):
        return lax.rem(y + (off + NY), NY)

    def pz(off):
        return lax.rem(z + (off + NZ), NZ)

    def rows(i, size, off=0, n=None):
        return pl.ds(pl.multiple_of(i * size + off, 16), size if n is None else n)

    def lanes(i):
        return pl.ds(pl.multiple_of(i * TB, TB), TB)

    msg = Messages(send_sem, recv_sem)

    barrier = pltpu.get_barrier_semaphore()
    partners = [("x", 1), ("x", -1), ("x", 2), ("y", 1), ("y", -1), ("y", 2), ("z", 1), ("z", -1), ("c", 0)]
    for ax, off in partners:
        pl.semaphore_signal(barrier, inc=1, device_id=dev(ax, off), device_id_type=MESH)

    xt[rows(x, DX), lanes(y)] = x_in[...]
    nc[1, rows(x, DX), lanes(y)] = c_in[...]
    gr[x] = g_in[...]
    pl.semaphore_wait(barrier, len(partners))

    class Gather:
        def __init__(self, ref, first, second):
            self.ref, self.a, self.b = ref, first, second
            self.n1, self.n2 = {}, {}

        def at(self, a, b, half=None):
            xi, yi = (px(a), py(b)) if self.a == "x" else (px(b), py(a))
            off, n = (0, DX) if half is None else HALF[half]
            return self.ref(rows(xi, DX, off, n), lanes(yi))

        def go(self, a, b, ax, off, half=None):
            ref = self.at(a, b, half)
            return msg.start(ref, ref, dev(ax, off))

        def first(self):
            self.m1 = [self.go(0, 0, self.a, 1), self.go(0, 0, self.a, -1)]

        def second(self, a):
            self.n1[a] = [self.go(a, 0, self.b, 1), self.go(a, 0, self.b, -1)]

        def first_forward(self):
            self.m1[0].wait_recv()
            m2p = self.go(-1, 0, self.a, 1, 0)
            self.m1[1].wait_recv()
            m2m = self.go(1, 0, self.a, -1, 1)
            self.m2 = [m2p, m2m]

        def first_done(self):
            for cp in self.m2:
                cp.wait_recv()

        def second_forward(self, a):
            self.n1[a][0].wait_recv()
            p = self.go(a, -1, self.b, 1, 0)
            self.n1[a][1].wait_recv()
            m = self.go(a, 1, self.b, -1, 1)
            self.n2[a] = [p, m]

        def second_done(self, a):
            for cp in self.n2[a]:
                cp.wait_recv()

    gx = Gather(lambda r, l: xt.at[r, l], "x", "y")
    gc = Gather(lambda r, l: nc.at[1, r, l], "y", "x")

    gain_msgs = [msg.start(g_in, gr.at[x], dev("x", off)) for off in (1, -1, 2)]
    a2a = [msg.start(w_in.at[d, py(off)], wa.at[y], dev("y", off)) for off in (1, -1, 2)]
    gx.first()
    gc.first()
    gx.second(0)
    gc.second(0)
    wa[y] = w_in[d, y]

    r_i = lax.broadcasted_iota(jnp.int32, (DZ, NY * RP), 0)
    c_i = lax.broadcasted_iota(jnp.int32, (DZ, NY * RP), 1)
    shift = jnp.where(r_i >= 3 * DC, 3, jnp.where(r_i >= 2 * DC, 2, jnp.where(r_i >= DC, 1, 0)))
    select = jnp.where(c_i == r_i + (RP - DC) * shift, 1.0, 0.0).astype(BF16)

    for cp in a2a:
        cp.wait_recv()
    w[d, rows(z, DZ)] = dot(select, wa[...].reshape(NY * RP, FP), 1, 0).astype(BF16)

    def w_at(off, sub):
        o, n = SUBS[sub]
        return w.at[d, rows(pz(off), DZ, o, n)]

    zp, zm, wc = {}, {}, []

    def z_send(s):
        for sub in (0, 1):
            if s < 3 or sub == 0:
                zp[s, sub] = msg.start(w_at(-s, sub), w_at(-s, sub), dev("z", 1))
            if s < 3 or sub == 1:
                zm[s, sub] = msg.start(w_at(s, sub), w_at(s, sub), dev("z", -1))

    def z_step(s):
        for sub in (0, 1):
            if (s, sub) in zp:
                zp[s, sub].wait_recv()
                if s < 2 or (s == 2 and sub == 0):
                    ref = w_at(-(s + 1), sub)
                    zp[s + 1, sub] = msg.start(ref, ref, dev("z", 1))
            if (s, sub) in zm:
                zm[s, sub].wait_recv()
                if s < 2 or (s == 2 and sub == 1):
                    ref = w_at(s + 1, sub)
                    zm[s + 1, sub] = msg.start(ref, ref, dev("z", -1))
            if (s, sub) in zp:
                ref = w_at(-(s + 1), sub)
                wc.append(msg.start(ref, ref, dev("c")))
            if (s, sub) in zm:
                ref = w_at(s + 1, sub)
                wc.append(msg.start(ref, ref, dev("c")))

    z_send(0)
    for sub in (0, 1):
        ref = w_at(0, sub)
        wc.append(msg.start(ref, ref, dev("c")))

    gx.first_forward()
    gc.first_forward()
    for a in (-1, 1):
        gx.second(a)
        gc.second(a)
    for cp in gain_msgs:
        cp.wait_recv()

    def spread_gain(i, carry):
        column = gr[i].T[:DX, 0:1]
        gcol[i] = jnp.broadcast_to(column, (DX, TB))
        return carry

    lax.fori_loop(0, NX, spread_gain, 0)

    def normalise(off):
        yi = py(off)

        def square(i, acc):
            v = xt[pl.ds(pl.multiple_of(i * 160, 16), 160), lanes(yi)].astype(F32)
            return acc + jnp.sum(v * v, axis=0, keepdims=True)

        total = lax.fori_loop(0, D // 160, square, jnp.zeros((1, TB), F32))
        inv = lax.rsqrt(total / D + EPS)
        if off == 0:
            inv_s[...] = inv

        def scale(i, carry):
            xi, k = i // 5, lax.rem(i, 5)
            r = pl.ds(pl.multiple_of(i * 160, 16), 160)
            v = xt[r, lanes(yi)].astype(F32) * inv
            nc[0, r, lanes(yi)] = (v * gcol[xi, pl.ds(pl.multiple_of(k * 160, 16), 160)]).astype(BF16)
            return carry

        lax.fori_loop(0, D // 160, scale, 0)

    gx.first_done()
    gx.second(2)
    gc.first_done()
    gc.second(2)
    normalise(0)
    gx.second_forward(0)
    gc.second_forward(0)
    z_step(0)
    for a in (-1, 1):
        gx.second_forward(a)
        gc.second_forward(a)
    z_step(1)
    gx.second_forward(2)
    gc.second_forward(2)
    normalise(1)
    normalise(-1)
    z_step(2)
    for a in (0, -1, 1, 2):
        gx.second_done(a)
    normalise(2)
    for a in (0, -1, 1, 2):
        gc.second_done(a)
    z_step(3)
    for cp in wc:
        cp.wait_recv()
    msg.drain()

    pre_s[...] = jnp.zeros_like(pre_s)
    dh_s[...] = jnp.zeros_like(dh_s)

    def up(i, carry):
        r = rows(i, DZ)
        pre_s[...] += dot(w[0, r], nc[0, r], 0, 0)
        dh_s[...] += dot(w[1, r], nc[1, r], 0, 0)
        return carry

    lax.fori_loop(0, NZ, up, 0)

    hd[0, pl.ds(FS, FP - FS)] = jnp.zeros((FP - FS, T), BF16)
    hd[1, pl.ds(FS, FP - FS)] = jnp.zeros((FP - FS, T), BF16)

    def act(i, acc):
        r = pl.ds(pl.multiple_of(i * 16, 16), 16)
        pre = pre_s[r]
        dpre = dh_s[r] * gelu_slope(pre)
        hd[1, r] = gelu_value(pre).astype(BF16)
        hd[0, r] = dpre.astype(BF16)
        return acc + jnp.sum(dpre * pre, axis=0, keepdims=True)

    md_s[...] = lax.fori_loop(0, FS // 16, act, jnp.zeros((1, T), F32))

    core = {}

    def grad_chunk(k):
        r = rows(pz(ZORDER[k]), DZ)
        xt[pl.ds(k * DZ, DZ)] = dot(nc[e, r], hd[e], 1, 1).astype(BF16)
        core[k] = msg.start(xt.at[pl.ds(k * DZ, DZ)], xr.at[k], dev("c"))
        g[k] = dot(nc[d, r], hd[d], 1, 1)

    zmsg = {}

    def z_reduce(s, k, p):
        for sub in (0, 1):
            if s == 0 and sub != p:
                continue
            o, n = SUBS[sub]
            r = pl.ds(o, n)
            val = g[k, r] + xr[k, r].astype(F32)
            if (p, s - 1, sub) in zmsg:
                zmsg[p, s - 1, sub].wait_recv()
                val = val + zr[p, s - 1, r].astype(F32)
            zs[p, s, r] = val.astype(BF16)
            zmsg[p, s, sub] = msg.start(zs.at[p, s, r], zr.at[p, s, r], dev("z", 1 - 2 * p))

    class Reduce:
        def __init__(self, ref, a, b, halves, r0, r1, q0, q1):
            self.ref, self.a, self.b, self.h = ref, a, b, halves
            self.r0, self.r1, self.q0, self.q1 = r0, r1, q0, q1
            self.p0, self.p1 = {}, {}

        def at(self, a, b):
            return (px(a), py(b)) if self.a == "x" else (px(b), py(a))

        def send0(self, b):
            i = ORDER.index(b)
            xi, yi = self.at(2, b)
            self.p0[b] = []
            for s in (0, 1):
                o, n = self.h[s]
                self.p0[b].append(msg.start(
                    self.ref.at[xi, yi, pl.ds(o, n)], self.r0.at[i, s, pl.ds(0, n)], dev(self.a, 1 - 2 * s)))

        def send1(self, b):
            i = ORDER.index(b)
            self.p1[b] = []
            for s in (0, 1):
                o, n = self.h[s]
                xi, yi = self.at(1 - 2 * s, b)
                self.p0[b][s].wait_recv()
                self.ref[xi, yi, pl.ds(o, n)] = (
                    self.ref[xi, yi, pl.ds(o, n)].astype(F32) + self.r0[i, s, pl.ds(0, n)].astype(F32)
                ).astype(BF16)
                self.p1[b].append(msg.start(self.ref.at[xi, yi], self.r1.at[i, s], dev(self.a, 1 - 2 * s)))

        def sum1(self, b):
            i = ORDER.index(b)
            xi, yi = self.at(0, b)
            for s in (0, 1):
                self.p1[b][s].wait_recv()
            return self.ref[xi, yi].astype(F32) + self.r1[i, 0].astype(F32) + self.r1[i, 1].astype(F32)

        def second0(self):
            xi, yi = self.at(0, 2)
            self.ref[xi, yi] = self.sum1(2).astype(BF16)
            self.m0 = []
            for s in (0, 1):
                o, n = self.h[s]
                self.m0.append(msg.start(
                    self.ref.at[xi, yi, pl.ds(o, n)], self.q0.at[s, pl.ds(0, n)], dev(self.b, 1 - 2 * s)))

        def second1(self):
            self.m1 = []
            for s in (0, 1):
                b = 1 - 2 * s
                xi, yi = self.at(0, b)
                o, n = self.h[s]
                total = self.sum1(b)
                self.m0[s].wait_recv()
                other = slice(n, None) if o == 0 else slice(0, o)
                self.ref[xi, yi, pl.ds(o, n)] = (
                    total[o:o + n] + self.q0[s, pl.ds(0, n)].astype(F32)).astype(BF16)
                so, sn = self.h[1 - s]
                self.ref[xi, yi, pl.ds(so, sn)] = total[other].astype(BF16)
                self.m1.append(msg.start(self.ref.at[xi, yi], self.q1.at[s], dev(self.b, b)))

        def result(self):
            total = self.sum1(0)
            for s in (0, 1):
                self.m1[s].wait_recv()
            return total + self.q1[0].astype(F32) + self.q1[1].astype(F32)

    rb = Reduce(br, "y", "x", HALF, b0, b1, bq0, bq1)
    rd = Reduce(dn, "x", "y", HALFE, d0, d1, dq0, dq1)

    def branch_block(off):
        xi = px(off)
        val = dot(w[1, rows(xi, DX)], hd[1], 1, 0).astype(BF16)
        for j in range(NY):
            br[xi, j] = val[:, j * TB:(j + 1) * TB]

    def normed_block(off):
        xi = px(off)
        val = dot(w[0, rows(xi, DX)], hd[0], 1, 0).astype(BF16)
        for j in range(NY):
            dn[xi, j, pl.ds(0, DX)] = val[:, j * TB:(j + 1) * TB]
            dn[xi, j, pl.ds(DX, EX)] = jnp.broadcast_to(
                md_s[:, j * TB:(j + 1) * TB], (EX, TB)).astype(BF16)

    grad_chunk(0)
    branch_block(2)
    rb.send0(2)
    normed_block(2)
    for b in ORDER:
        rd.send0(b)
    core[0].wait_recv()
    z_reduce(0, 0, 0)
    z_reduce(0, 0, 1)
    branch_block(1)
    rb.send0(1)
    branch_block(-1)
    rb.send0(-1)
    branch_block(0)
    rb.send0(0)
    grad_chunk(1)
    grad_chunk(2)
    normed_block(1)
    normed_block(-1)
    rb.send1(2)
    rd.send1(2)
    for k in (1, 2):
        core[k].wait_recv()
    z_reduce(1, 1, 0)
    z_reduce(1, 2, 1)
    normed_block(0)
    for b in (1, -1, 0):
        rb.send1(b)
        rd.send1(b)
    for k in (3, 4):
        grad_chunk(k)
    rb.second0()
    rd.second0()
    for k in (3, 4):
        core[k].wait_recv()
    z_reduce(2, 3, 0)
    z_reduce(2, 4, 1)
    for k in (5, 6, 7):
        grad_chunk(k)
    rb.second1()
    rd.second1()
    for k in (5, 6):
        core[k].wait_recv()
    z_reduce(3, 5, 0)
    z_reduce(3, 6, 1)

    xf = x_in[...].astype(F32)
    out_ref[...] = (xf + rb.result()).astype(BF16)
    total = rd.result()
    dnorm = total[:DX]
    inv = inv_s[...]
    mean_dot = total[DX:DX + 1] / D
    unit = xf * inv
    dtok_ref[...] = (
        c_in[...].astype(F32) + inv * (dnorm * gcol[x] - unit * mean_dot)
    ).astype(BF16)
    gg_ref[...] = jnp.sum(dnorm * unit, axis=1, keepdims=True)

    core[7].wait_recv()
    for p in (0, 1):
        for sub in (0, 1):
            zmsg[p, 3, sub].wait_recv()
    final = (
        g[7] + xr[7].astype(F32) + zr[0, 3].astype(F32) + zr[1, 3].astype(F32)
    ).astype(BF16)
    stage[...] = dot(select, final, 0, 0).astype(BF16).reshape(NY, RP, FP)
    back = [msg.start(stage.at[py(off)], ga.at[d, y], dev("y", off)) for off in (1, -1, 2)]
    ga[d, y] = stage[y]
    hand = [msg.start(ga.at[d, y], ga.at[d, y], dev("c"))]
    for cp, off in zip(back, (1, -1, 2)):
        cp.wait_recv()
        ref = ga.at[d, py(-off)]
        hand.append(msg.start(ref, ref, dev("c")))
    for cp in hand:
        cp.wait_recv()
    gw_ref[...] = ga[...]
    msg.drain()


def vm(shape, dtype=BF16):
    return pltpu.VMEM(shape, dtype)


def block(xt, ct, w, g):
    spec = pl.BlockSpec(memory_space=pltpu.VMEM)
    return pl.pallas_call(
        kernel,
        out_shape=(
            jax.ShapeDtypeStruct((DX, TB), BF16),
            jax.ShapeDtypeStruct((DX, TB), BF16),
            jax.ShapeDtypeStruct((2, NY, RP, FP), BF16),
            jax.ShapeDtypeStruct((DX, 1), F32),
        ),
        in_specs=[spec] * 4,
        out_specs=(spec,) * 4,
        scratch_shapes=[
            vm((D, T)),
            vm((2, D, T)),
            vm((2, D, FP)),
            vm((NY, RP, FP)),
            vm((NX, 8, 896), F32),
            vm((NX, DX, TB), F32),
            vm((1, TB), F32),
            vm((FP, T), F32),
            vm((FP, T), F32),
            vm((2, FP, T)),
            vm((1, T), F32),
            vm((NZ, DZ, FP), F32),
            vm((NZ, DZ, FP)),
            vm((2, 4, DZ, FP)),
            vm((2, 4, DZ, FP)),
            vm((NX, NY, DX, TB)),
            vm((NX, NY, DE, TB)),
            vm((4, 2, 400, TB)),
            vm((4, 2, DX, TB)),
            vm((2, 400, TB)),
            vm((2, DX, TB)),
            vm((4, 2, 416, TB)),
            vm((4, 2, DE, TB)),
            vm((2, 416, TB)),
            vm((2, DE, TB)),
            vm((NY, RP, FP)),
            vm((2, NY, RP, FP)),
            pltpu.SemaphoreType.DMA((N_MESSAGES,)),
            pltpu.SemaphoreType.DMA((N_MESSAGES,)),
            pltpu.SemaphoreType.DMA,
        ],
        compiler_params=pltpu.CompilerParams(
            collective_id=0, has_side_effects=True, vmem_limit_bytes=60 * 2**20
        ),
    )(xt, ct, w, g)


def on_device(tokens, gain, w_up, w_down, cotangent):
    up = w_up.reshape(DC, NY, FS).transpose(1, 0, 2)
    down = w_down.reshape(NY, FS, DC).transpose(0, 2, 1)
    w = jnp.pad(jnp.stack([up, down]), ((0, 0), (0, 0), (0, RP - DC), (0, FP - FS)))
    g = jnp.broadcast_to(jnp.pad(gain.astype(F32), (0, 896 - DX))[None], (8, 896))
    out_t, dtok_t, gw, gg = block(tokens.T, cotangent.T, w, g)
    scale = TOK ** (-0.5)
    gw = gw[:, :, :DC, :FS].astype(F32) * scale
    grad_up = gw[0].transpose(1, 0, 2).reshape(DC, NY * FS)
    grad_down = gw[1].transpose(0, 2, 1).reshape(NY * FS, DC)
    grad_gain = lax.psum(gg[:, 0], ("col", "depth")) * scale
    return out_t.T, dtok_t.T, grad_up, grad_down, grad_gain


def solution(mesh):
    in_specs = (
        P(("depth", "col"), "row"),
        P("row"),
        P("col", "row"),
        P("row", "col"),
        P(("depth", "col"), "row"),
    )
    out_specs = (
        P(("depth", "col"), "row"),
        P(("depth", "col"), "row"),
        P("col", "row"),
        P("row", "col"),
        P("row"),
    )
    return jax.shard_map(
        on_device, mesh=mesh, in_specs=in_specs, out_specs=out_specs, check_vma=False
    )
```

time: 752 us -> 261 us (0.35)
  waiting for transfers between devices: 455 us -> 0 us
  Pallas kernels: 0 us -> 123 us
  matrix products: 52 us -> 0 us
  blocking collectives: 168 us -> 124 us
  local copies, waits for them, and re-layouts: 42.5 us -> 8.59 us
  between operations: 14.9 us -> 0.73 us
  starting transfers between devices: 12.5 us -> 0 us
    all_gather x4 -> x0, waiting for transfers between devices: 363 us -> none  [the longest x1 120 us: on_device(): lax.all_gather(hidden, 'col', axis=0, tiled=True)]
    pallas_call x0 -> x1, Pallas kernels: none -> 123 us  [block(): pl.pallas_call(kernel, out_shape=(jax.ShapeDtypeStruct((DX, TB), BF16), j...]
    dot_general x6 -> x0, matrix products: 52 us -> none  [the longest x5 43.1 us: contract(): lax.dot_general(left, right, (((left_dim,), (right_dim,)), ((), ())), pre...]
    unnamed x9 -> x0, waiting for transfers between devices: 51.5 us -> none
    all_to_all x2 -> x0, waiting for transfers between devices: 40.9 us -> none  [the longest x1 26.6 us: on_device(): lax.all_to_all(full_cot, 'col', split_axis=1, concat_axis=0, tiled=True)]
    unnamed x23 -> x8, local copies, waits for them, and re-layouts: 40.2 us -> 1.37 us
    all_gather x2 -> x0, blocking collectives: 24.2 us -> none  [the longest x1 12.7 us: on_device(): lax.all_gather(tokens, 'row', axis=1, tiled=True)]
    all_to_all x2 -> x0, starting transfers between devices: 11.8 us -> none  [the longest x1 6.51 us: on_device(): lax.all_to_all(normed, 'col', split_axis=1, concat_axis=0, tiled=True)]
  transfers between devices with their start and end apart: 9 -> 0, of which waited for: 8 -> 0; matrix products, arithmetic and copies ran while one was open for 9% -> 0% of each run, Pallas kernels for 0% -> 0%
where the time goes in v1:
time: 261 us
  blocking collectives  124 us (48%)
  Pallas kernels  123 us (47%)
  local copies, waits for them, and re-layouts  8.59 us (3%)
  other arithmetic  5.02 us (2%)
    psum x1, blocking collectives, on_device(): grad_gain = lax.psum(gg[:, 0], ('col', 'depth')) * scale  124 us
    pallas_call x1, Pallas kernels, block(): pl.pallas_call(kernel, out_shape=(jax.ShapeDtypeStruct((DX, TB), BF16), j...  123 us

profile of v1, /device:TPU:1, one launch (start us, length us, event | category | flops | bytes accessed | tf_op | source)
XLA Modules:
  0.0 261.0 jit_solution(1031704787576847685)
XLA Ops:
  0.6 0.0 copy-start
  0.6 0.7 pad_convert_fusion
  1.4 0.6 broadcast_in_dim.2.g_in
  2.0 1.6 reshape.23
  3.6 0.1 copy.17
  3.7 0.0 copy-done
  3.7 0.6 reshape.24
  4.3 0.1 copy.16
  4.4 1.1 fusion.5.w_in
  5.5 123.1 %shard_map.92 = (bf16[800,128]{1,0:T(8,128)(2,1)}, bf16[800,128]{1,0:T(8,128)(2,1)}, bf16[2,4,112,512]{3,2,1,0:T(8,128)(2,1)}, f32[800,1]{1,0:T(8,128)}) custom-call(bf16[800,128]{1,0:T(8,128)(2,1)} %bitcast.30, bf16[800,128]{1,0:T(8,128)(2,1)} %bitcast.31, bf16[2,4,112,512]{3,2,1,0:T(8,128)(2,1)} %fusion.5.w_in, f32[8,896]{1,0:T(8,128)} %broadcast_in_dim.2.g_in), custom_call_target="tpu_custom_call" | custom-call | tf_op jit(solution)/shard_map/pallas_call | solution.py:503
  128.6 1.2 reduce
  129.8 123.6 %psum.7 = f32[800]{0:T(1024)S(1)} all-reduce(f32[800]{0:T(1024)S(1)} %reduce), channel_id=1, replica_groups=mesh['row'=4,'col'=32,'depth'=2] {'col','depth'}, use_global_device_ids=true, to_apply=%region_0.1 | all-reduce | flops 800 | bytes 6400 | tf_op jit(solution)/shard_map/psum | solution.py:561
  253.4 0.6 broadcast_multiply_fusion
  254.0 1.4 convert_multiply_fusion
  255.4 0.1 slice_bitcast_fusion
  255.5 0.5 copy.13
  256.1 1.5 reshape.26
  257.6 0.0 copy-start.2
  257.6 0.5 copy.12
  258.1 1.5 reshape.25
  259.7 0.0 copy-done.2
  259.7 0.7 copy.20
  260.3 0.0 copy-done.1
  260.3 0.7 copy.21
  (1 shorter events, 0.0 us)
Async XLA Ops:
  0.6 3.0 %copy-start = (bf16[1600,100]{0,1:T(8,128)(2,1)S(1)}, bf16[1600,100]{0,1:T(8,128)(2,1)}, u32[]{:S(2)}) copy-start(bf16[1600,100]{0,1:T(8,128)(2,1)} %param.8) | copy-start | bytes 960004
  257.6 2.1 copy-start.2
  257.6 2.7 %copy-start.1 = (bf16[800,128]{1,0:T(8,128)(2,1)S(1)}, bf16[800,128]{1,0:T(8,128)(2,1)}, u32[]{:S(2)}) copy-start(bf16[800,128]{1,0:T(8,128)(2,1)} %get-tuple-element.10) | copy-start | bytes 614404

commit v2 on v1

--- a/solution.py
+++ b/solution.py
@@ -23,11 +23,14 @@
 RP = 112
 EX = 16
 DE = DX + EX
-SUBS = ((0, 208), (208, 192))
+FM = 384
+ZP = 432
+SUBS = ((0, 208), (208, 224))
 HALF = ((0, 400), (400, 400))
 HALFE = ((0, 400), (400, 416))
 ORDER = (2, 1, -1, 0)
 ZORDER = (4, 3, -3, 2, -2, 1, -1, 0)
+SCALE = TOK ** (-0.5)
 
 
 def gelu_value(pre):
@@ -71,10 +74,10 @@
 
 
 def kernel(
-    x_in, c_in, w_in, g_in,
-    out_ref, dtok_ref, gw_ref, gg_ref,
-    xt, nc, w, wa, gr, gcol, inv_s, pre_s, dh_s, hd, md_s, g, xr, zs, zr,
-    br, dn, b0, b1, bq0, bq1, d0, d1, dq0, dq1, stage, ga,
+    x_in, c_in, up_in, down_in, g_in,
+    out_hbm, dtok_hbm, gu_hbm, gd_hbm, gg_ref,
+    xo, co, ws, w_in, wz, out_ref, dtok_ref, gu_ref, gd_ref, xt, nc, w, wa, gr, gcol, inv_s, pre_s, dh_s, hd, md_s, gs, g, xr, zs, zr,
+    br, dn, b0, b1, bq0, bq1, d0, d1, dq0, dq1, stage, ga, ggp, ggr, ggx, ggy, ggz, ggc,
     send_sem, recv_sem, copy_sem,
 ):
     x = lax.axis_index("row")
@@ -117,9 +120,32 @@
     for ax, off in partners:
         pl.semaphore_signal(barrier, inc=1, device_id=dev(ax, off), device_id_type=MESH)
 
-    xt[rows(x, DX), lanes(y)] = x_in[...]
-    nc[1, rows(x, DX), lanes(y)] = c_in[...]
-    gr[x] = g_in[...]
+    loads = [pltpu.make_async_copy(x_in, xo, copy_sem.at[0]), pltpu.make_async_copy(c_in, co, copy_sem.at[1])]
+    for cp in loads:
+        cp.start()
+
+    @pl.when(d == 0)
+    def _():
+        cp = pltpu.make_async_copy(up_in, ws, copy_sem.at[2])
+        cp.start()
+        cp.wait()
+
+    @pl.when(d == 1)
+    def _():
+        cp = pltpu.make_async_copy(down_in, ws, copy_sem.at[2])
+        cp.start()
+        cp.wait()
+
+    w_in[...] = jnp.zeros_like(w_in)
+    for j in range(NY):
+        w_in[j, pl.ds(0, DC), pl.ds(0, FS)] = ws[:, j * FS:(j + 1) * FS]
+    for cp in loads:
+        cp.wait()
+    xt[rows(x, DX), lanes(y)] = xo[...]
+    nc[1, rows(x, DX), lanes(y)] = co[...]
+    gain_own = g_in[...].astype(F32)
+    gr[x] = jnp.zeros_like(gr[0])
+    gr[x, :, pl.ds(0, DX)] = jnp.broadcast_to(gain_own, (8, DX))
     pl.semaphore_wait(barrier, len(partners))
 
     class Gather:
@@ -167,13 +193,13 @@
     gx = Gather(lambda r, l: xt.at[r, l], "x", "y")
     gc = Gather(lambda r, l: nc.at[1, r, l], "y", "x")
 
-    gain_msgs = [msg.start(g_in, gr.at[x], dev("x", off)) for off in (1, -1, 2)]
-    a2a = [msg.start(w_in.at[d, py(off)], wa.at[y], dev("y", off)) for off in (1, -1, 2)]
+    gain_msgs = [msg.start(gr.at[x], gr.at[x], dev("x", off)) for off in (1, -1, 2)]
+    a2a = [msg.start(w_in.at[py(off)], wa.at[y], dev("y", off)) for off in (1, -1, 2)]
     gx.first()
     gc.first()
     gx.second(0)
     gc.second(0)
-    wa[y] = w_in[d, y]
+    wa[y] = w_in[y]
 
     r_i = lax.broadcasted_iota(jnp.int32, (DZ, NY * RP), 0)
     c_i = lax.broadcasted_iota(jnp.int32, (DZ, NY * RP), 1)
@@ -182,11 +208,36 @@
 
     for cp in a2a:
         cp.wait_recv()
-    w[d, rows(z, DZ)] = dot(select, wa[...].reshape(NY * RP, FP), 1, 0).astype(BF16)
+    own = dot(select, wa[...].reshape(NY * RP, FP), 1, 0)
+    w[d, rows(z, DZ)] = own.astype(BF16)
+
+    def pack(ref, i, val):
+        tail = jnp.concatenate([val[:, FM:], jnp.zeros((FP - DZ, FP - FM), F32)], axis=0).T[:16]
+        ref[i, pl.ds(0, DZ)] = val[:, :FM].astype(ref.dtype)
+        ref[i, pl.ds(DZ, 16)] = tail[:, :FM].astype(ref.dtype)
+        ref[i, pl.ds(DZ + 16, 16), pl.ds(0, FP - FM)] = tail[:, FM:].astype(ref.dtype)
+
+    def tail_of(val):
+        tail = jnp.concatenate([val[DZ:DZ + 16], val[DZ + 16:, :FP - FM]], axis=1)
+        tail = jnp.concatenate([tail, jnp.zeros((FP - FM - 16, FP), F32)], axis=0)
+        return tail.T[:DZ]
+
+    wz[z, pl.ds(DZ + 16, 16), :] = jnp.zeros((16, FM), BF16)
+    pack(wz, z, own)
 
     def w_at(off, sub):
         o, n = SUBS[sub]
-        return w.at[d, rows(pz(off), DZ, o, n)]
+        return wz.at[pz(off), pl.ds(o, n)]
+
+    def hand(off):
+        ref = w.at[d, rows(pz(off), DZ)]
+        wc.append(msg.start(ref, ref, dev("c")))
+
+    def unpack(off):
+        r = rows(pz(off), DZ)
+        w[d, r, pl.ds(0, FM)] = wz[pz(off), pl.ds(0, DZ)]
+        w[d, r, pl.ds(FM, FP - FM)] = tail_of(wz[pz(off)].astype(F32)).astype(BF16)
+        hand(off)
 
     zp, zm, wc = {}, {}, []
 
@@ -209,17 +260,12 @@
                 if s < 2 or (s == 2 and sub == 1):
                     ref = w_at(s + 1, sub)
                     zm[s + 1, sub] = msg.start(ref, ref, dev("z", -1))
-            if (s, sub) in zp:
-                ref = w_at(-(s + 1), sub)
-                wc.append(msg.start(ref, ref, dev("c")))
-            if (s, sub) in zm:
-                ref = w_at(s + 1, sub)
-                wc.append(msg.start(ref, ref, dev("c")))
+        unpack(s + 1)
+        if s < 3:
+            unpack(-(s + 1))
 
     z_send(0)
-    for sub in (0, 1):
-        ref = w_at(0, sub)
-        wc.append(msg.start(ref, ref, dev("c")))
+    hand(0)
 
     gx.first_forward()
     gc.first_forward()
@@ -309,12 +355,59 @@
     md_s[...] = lax.fori_loop(0, FS // 16, act, jnp.zeros((1, T), F32))
 
     core = {}
+    ggr[...] = jnp.zeros_like(ggr)
+    g[:, pl.ds(DZ + 16, 16), :] = jnp.zeros((NZ, 16, FM), F32)
+    ones = jnp.ones((8, FP), BF16)
+
+    def fold(k):
+        core[k].wait_recv()
+        zc = pz(ZORDER[k])
+        total = gs[k] + xr[k].astype(F32)
+        pack(g, k, total)
+        v = total * w[d, rows(zc, DZ)].astype(F32)
+        high = v.astype(BF16)
+        low = (v - high.astype(F32)).astype(BF16)
+        ggr[:, pl.ds(0, DZ)] = dot(ones, high, 1, 1) + dot(ones, low, 1, 1)
+        for j in range(4):
+            ggp[zc // 2, pl.ds(lax.rem(zc, 2) * 4 + j, 1), :] = ggr[0:1, j * TB:(j + 1) * TB]
+
+    def gain_x():
+        return [msg.start(ggp.at[px(off)], ggx.at[i], dev("x", off)) for i, off in enumerate((1, -1, 2))]
+
+    def gain_y(cps):
+        for cp in cps:
+            cp.wait_recv()
+        ggy[0] = ggp[x] + ggx[0] + ggx[1] + ggx[2]
+        return [msg.start(ggy.at[0], ggy.at[1 + i], dev("y", off)) for i, off in enumerate((1, -1, 2))]
+
+    def gain_z(cps):
+        for cp in cps:
+            cp.wait_recv()
+        ggz[0] = ggy[0] + ggy[1] + ggy[2] + ggy[3]
+        return [msg.start(ggz.at[0], ggz.at[1 + p], dev("z", 1 - 2 * p)) for p in (0, 1)]
+
+    def gain_ring(cps, s):
+        for cp in cps:
+            cp.wait_recv()
+        return [
+            msg.start(ggz.at[2 * s - 1 + p], ggz.at[2 * s + 1 + p], dev("z", 1 - 2 * p))
+            for p in ((0, 1) if s < 3 else (0,))
+        ]
+
+    def gain_c(cps):
+        for cp in cps:
+            cp.wait_recv()
+        total = ggz[0]
+        for i in range(NZ - 1):
+            total = total + ggz[1 + i]
+        ggc[0] = total
+        return [msg.start(ggc.at[0], ggc.at[1], dev("c"))]
 
     def grad_chunk(k):
         r = rows(pz(ZORDER[k]), DZ)
         xt[pl.ds(k * DZ, DZ)] = dot(nc[e, r], hd[e], 1, 1).astype(BF16)
         core[k] = msg.start(xt.at[pl.ds(k * DZ, DZ)], xr.at[k], dev("c"))
-        g[k] = dot(nc[d, r], hd[d], 1, 1)
+        gs[k] = dot(nc[d, r], hd[d], 1, 1)
 
     zmsg = {}
 
@@ -324,7 +417,7 @@
                 continue
             o, n = SUBS[sub]
             r = pl.ds(o, n)
-            val = g[k, r] + xr[k, r].astype(F32)
+            val = g[k, r]
             if (p, s - 1, sub) in zmsg:
                 zmsg[p, s - 1, sub].wait_recv()
                 val = val + zr[p, s - 1, r].astype(F32)
@@ -421,96 +514,129 @@
     normed_block(2)
     for b in ORDER:
         rd.send0(b)
-    core[0].wait_recv()
+    fold(0)
     z_reduce(0, 0, 0)
     z_reduce(0, 0, 1)
+    grad_chunk(1)
+    grad_chunk(2)
     branch_block(1)
     rb.send0(1)
     branch_block(-1)
     rb.send0(-1)
+    fold(1)
+    fold(2)
     branch_block(0)
     rb.send0(0)
-    grad_chunk(1)
-    grad_chunk(2)
     normed_block(1)
     normed_block(-1)
+    z_reduce(1, 1, 0)
+    z_reduce(1, 2, 1)
     rb.send1(2)
     rd.send1(2)
-    for k in (1, 2):
-        core[k].wait_recv()
-    z_reduce(1, 1, 0)
-    z_reduce(1, 2, 1)
+    grad_chunk(3)
+    grad_chunk(4)
     normed_block(0)
     for b in (1, -1, 0):
         rb.send1(b)
         rd.send1(b)
-    for k in (3, 4):
-        grad_chunk(k)
-    rb.second0()
-    rd.second0()
-    for k in (3, 4):
-        core[k].wait_recv()
+    fold(3)
+    fold(4)
     z_reduce(2, 3, 0)
     z_reduce(2, 4, 1)
     for k in (5, 6, 7):
         grad_chunk(k)
-    rb.second1()
-    rd.second1()
-    for k in (5, 6):
-        core[k].wait_recv()
+    rb.second0()
+    rd.second0()
+    for k in (5, 6, 7):
+        fold(k)
+    gain = gain_x()
     z_reduce(3, 5, 0)
     z_reduce(3, 6, 1)
-
-    xf = x_in[...].astype(F32)
+    gain = gain_y(gain)
+    rb.second1()
+    gain = gain_z(gain)
+    rd.second1()
+    gain = gain_ring(gain, 1)
+
+    xf = xo[...].astype(F32)
     out_ref[...] = (xf + rb.result()).astype(BF16)
+    stores = [pltpu.make_async_copy(out_ref, out_hbm, copy_sem.at[0])]
+    stores[0].start()
+    gain = gain_ring(gain, 2)
     total = rd.result()
     dnorm = total[:DX]
     inv = inv_s[...]
     mean_dot = total[DX:DX + 1] / D
     unit = xf * inv
     dtok_ref[...] = (
-        c_in[...].astype(F32) + inv * (dnorm * gcol[x] - unit * mean_dot)
+        co[...].astype(F32) + inv * (dnorm * gcol[x] - unit * mean_dot)
     ).astype(BF16)
-    gg_ref[...] = jnp.sum(dnorm * unit, axis=1, keepdims=True)
-
-    core[7].wait_recv()
+    stores.append(pltpu.make_async_copy(dtok_ref, dtok_hbm, copy_sem.at[1]))
+    stores[1].start()
+    gain = gain_ring(gain, 3)
+
     for p in (0, 1):
         for sub in (0, 1):
             zmsg[p, 3, sub].wait_recv()
-    final = (
-        g[7] + xr[7].astype(F32) + zr[0, 3].astype(F32) + zr[1, 3].astype(F32)
-    ).astype(BF16)
+    final = g[7] + zr[0, 3].astype(F32) + zr[1, 3].astype(F32)
+    final = jnp.concatenate([final[:DZ], tail_of(final)], axis=1).astype(BF16)
     stage[...] = dot(select, final, 0, 0).astype(BF16).reshape(NY, RP, FP)
     back = [msg.start(stage.at[py(off)], ga.at[d, y], dev("y", off)) for off in (1, -1, 2)]
     ga[d, y] = stage[y]
-    hand = [msg.start(ga.at[d, y], ga.at[d, y], dev("c"))]
+    hands = [msg.start(ga.at[d, y], ga.at[d, y], dev("c"))]
+    gain = gain_c(gain)
     for cp, off in zip(back, (1, -1, 2)):
         cp.wait_recv()
         ref = ga.at[d, py(-off)]
-        hand.append(msg.start(ref, ref, dev("c")))
-    for cp in hand:
+        hands.append(msg.start(ref, ref, dev("c")))
+    for cp in hands:
         cp.wait_recv()
-    gw_ref[...] = ga[...]
+    for i, ref in enumerate((gu_ref, gd_ref)):
+        for j in range(NY):
+            ref[:, pl.ds(j * FS, FS)] = ga[i, j][:DC, :FS]
+    for i, (ref, hbm) in enumerate(((gu_ref, gu_hbm), (gd_ref, gd_hbm))):
+        stores.append(pltpu.make_async_copy(ref, hbm, copy_sem.at[2 + i]))
+        stores[2 + i].start()
+    for cp in gain:
+        cp.wait_recv()
+    total = jnp.where(d == 0, ggc[0], ggc[1]) * SCALE
+    for i in (0, 1):
+        row = jnp.concatenate([total[4 * i + j:4 * i + j + 1] for j in range(4)], axis=1)
+        gg_ref[:, pl.ds(i * DZ, DZ)] = row[:, :DZ]
+    gg_ref[...] = gg_ref[...] / gain_own
     msg.drain()
+    for cp in stores:
+        cp.wait()
 
 
 def vm(shape, dtype=BF16):
     return pltpu.VMEM(shape, dtype)
 
 
-def block(xt, ct, w, g):
+def block(x, c, up, down, g):
     spec = pl.BlockSpec(memory_space=pltpu.VMEM)
+    anywhere = pl.BlockSpec(memory_space=pl.ANY)
     return pl.pallas_call(
         kernel,
         out_shape=(
             jax.ShapeDtypeStruct((DX, TB), BF16),
             jax.ShapeDtypeStruct((DX, TB), BF16),
-            jax.ShapeDtypeStruct((2, NY, RP, FP), BF16),
-            jax.ShapeDtypeStruct((DX, 1), F32),
+            jax.ShapeDtypeStruct((DC, NY * FS), BF16),
+            jax.ShapeDtypeStruct((DC, NY * FS), BF16),
+            jax.ShapeDtypeStruct((1, DX), F32),
         ),
-        in_specs=[spec] * 4,
-        out_specs=(spec,) * 4,
+        in_specs=[anywhere] * 4 + [spec],
+        out_specs=(anywhere,) * 4 + (spec,),
         scratch_shapes=[
+            vm((DX, TB)),
+            vm((DX, TB)),
+            vm((DC, NY * FS)),
+            vm((NY, RP, FP)),
+            vm((NZ, ZP, FM)),
+            vm((DX, TB)),
+            vm((DX, TB)),
+            vm((DC, NY * FS)),
+            vm((DC, NY * FS)),
             vm((D, T)),
             vm((2, D, T)),
             vm((2, D, FP)),
@@ -523,9 +649,10 @@
             vm((2, FP, T)),
             vm((1, T), F32),
             vm((NZ, DZ, FP), F32),
+            vm((NZ, ZP, FM), F32),
             vm((NZ, DZ, FP)),
-            vm((2, 4, DZ, FP)),
-            vm((2, 4, DZ, FP)),
+            vm((2, 4, ZP, FM)),
+            vm((2, 4, ZP, FM)),
             vm((NX, NY, DX, TB)),
             vm((NX, NY, DE, TB)),
             vm((4, 2, 400, TB)),
@@ -538,28 +665,29 @@
             vm((2, DE, TB)),
             vm((NY, RP, FP)),
             vm((2, NY, RP, FP)),
+            vm((NX, 8, TB), F32),
+            vm((8, FP), F32),
+            vm((3, 8, TB), F32),
+            vm((4, 8, TB), F32),
+            vm((NZ, 8, TB), F32),
+            vm((2, 8, TB), F32),
             pltpu.SemaphoreType.DMA((N_MESSAGES,)),
             pltpu.SemaphoreType.DMA((N_MESSAGES,)),
-            pltpu.SemaphoreType.DMA,
+            pltpu.SemaphoreType.DMA((4,)),
         ],
         compiler_params=pltpu.CompilerParams(
             collective_id=0, has_side_effects=True, vmem_limit_bytes=60 * 2**20
         ),
-    )(xt, ct, w, g)
+    )(x, c, up, down, g)
 
 
 def on_device(tokens, gain, w_up, w_down, cotangent):
-    up = w_up.reshape(DC, NY, FS).transpose(1, 0, 2)
-    down = w_down.reshape(NY, FS, DC).transpose(0, 2, 1)
-    w = jnp.pad(jnp.stack([up, down]), ((0, 0), (0, 0), (0, RP - DC), (0, FP - FS)))
-    g = jnp.broadcast_to(jnp.pad(gain.astype(F32), (0, 896 - DX))[None], (8, 896))
-    out_t, dtok_t, gw, gg = block(tokens.T, cotangent.T, w, g)
-    scale = TOK ** (-0.5)
-    gw = gw[:, :, :DC, :FS].astype(F32) * scale
-    grad_up = gw[0].transpose(1, 0, 2).reshape(DC, NY * FS)
-    grad_down = gw[1].transpose(0, 2, 1).reshape(NY * FS, DC)
-    grad_gain = lax.psum(gg[:, 0], ("col", "depth")) * scale
-    return out_t.T, dtok_t.T, grad_up, grad_down, grad_gain
+    out, d_tokens, grad_up, grad_down, grad_gain = block(
+        tokens.T, cotangent.T, w_up, w_down.T, gain.reshape(1, DX))
+    return (
+        out.T, d_tokens.T, grad_up.astype(F32) * SCALE, grad_down.T.astype(F32) * SCALE,
+        grad_gain.reshape(DX),
+    )
 
 
 def solution(mesh):

time: 261 us -> 127 us (0.49)
  blocking collectives: 124 us -> 0 us
  local copies, waits for them, and re-layouts: 8.59 us -> 3.62 us
  Pallas kernels: 123 us -> 119 us
    psum x1 -> x0, blocking collectives: 124 us -> none  [on_device(): grad_gain = lax.psum(gg[:, 0], ('col', 'depth')) * scale]
    reshape x6 -> x1, local copies, waits for them, and re-layouts: 5.41 us -> 1.26 us  [on_device(): gain.reshape(1, DX)]
    pallas_call x1, Pallas kernels: 123 us -> 119 us  [block(): pl.pallas_call(kernel, out_shape=(jax.ShapeDtypeStruct((DX, TB), BF16), j...]
where the time goes in v2:
time: 127 us
  Pallas kernels  119 us (94%)
  local copies, waits for them, and re-layouts  3.62 us (3%)
  other arithmetic  2.91 us (2%)
    pallas_call x1, Pallas kernels, block(): pl.pallas_call(kernel, out_shape=(jax.ShapeDtypeStruct((DX, TB), BF16), j...  119 us

profile of v2, /device:TPU:1, one launch (start us, length us, event | category | flops | bytes accessed | tf_op | source)
XLA Modules:
  0.0 126.6 jit_solution(15121478533062747252)
XLA Ops:
  0.6 1.3 reshape.16.g_in
  1.9 119.4 %shard_map.92 = (bf16[800,128]{1,0:T(8,128)(2,1)}, bf16[800,128]{1,0:T(8,128)(2,1)}, bf16[100,1600]{1,0:T(8,128)(2,1)}, bf16[100,1600]{1,0:T(8,128)(2,1)}, f32[1,800]{1,0:T(1,128)}) custom-call(bf16[800,128]{1,0:T(8,128)(2,1)} %bitcast.8, bf16[800,128]{1,0:T(8,128)(2,1)} %bitcast.9, bf16[100,1600]{1,0:T(8,128)(2,1)} %up_in.1, bf16[100,1600]{1,0:T(8,128)(2,1)} %bitcast.7, ...), custom_call_target="tpu_custom_call" | custom-call | tf_op jit(solution)/shard_map/pallas_call | solution.py:619
  121.3 0.0 copy-start.1
  121.3 2.3 %multiply_bitcast_fusion = (f32[1600,100]{0,1:T(8,128)}, f32[100,1600]{1,0:T(8,128)}) fusion(bf16[100,1600]{1,0:T(8,128)(2,1)} %get-tuple-element.13, bf16[100,1600]{1,0:T(8,128)(2,1)} %get-tuple-element.12), kind=kLoop, calls=%fused_computation | loop fusion | flops 640000 | bytes 1920000 | tf_op jit(solution)/shard_map/mul | solution.py:688
  123.6 0.0 copy-start.2
  123.6 0.7 copy-done.2
  124.3 0.6 reduce
  124.9 0.0 copy-done.1
  124.9 0.0 copy-start
  124.9 0.7 copy.12
  125.6 0.3 copy-done
  125.9 0.7 copy.13
Async XLA Ops:
  121.3 3.6 %copy-start.1 = (bf16[800,128]{1,0:T(8,128)(2,1)S(1)}, bf16[800,128]{1,0:T(8,128)(2,1)}, u32[]{:S(2)}) copy-start(bf16[800,128]{1,0:T(8,128)(2,1)} %get-tuple-element.10) | copy-start | bytes 614404
  123.6 0.7 copy-start.2
  124.9 1.0 copy-start

commit v3 on v2

--- a/solution.py
+++ b/solution.py
@@ -70,13 +70,29 @@
         self.live = []
 
 
-N_MESSAGES = 176
+N_MESSAGES = 224
+
+SCHEDULE = (
+    ("B", 2), ("N", 2), ("G", 0), ("b0", 2), ("N", 1), ("B", 1), ("b0", 1), ("B", -1), ("N", -1), ("b0", -1),
+    ("d0", 2), ("G", 1), ("F", 0), ("Z", 0, 0, 0), ("Z", 0, 1, 1), ("Z", 0, 0, 2), ("G", 2), ("b1", 2, 0),
+    ("b1", 2, 1), ("B", 0), ("G", 3), ("G", 4), ("b1", 1, 1), ("d1", 2, 0), ("d1", 2, 1), ("Z", 0, 1, 3), ("F", 1),
+    ("F", 2), ("Z", 1, 1, 0), ("Z", 1, 0, 0), ("Z", 1, 1, 1), ("Z", 1, 0, 1), ("G", 7), ("b1", -1, 1), ("b1", -1, 0),
+    ("G", 5), ("Z", 1, 0, 2), ("b1", 1, 0), ("Z", 1, 1, 2), ("d0", -1), ("F", 3), ("b0", 0), ("N", 0), ("G", 6),
+    ("Z", 2, 0, 0), ("F", 4), ("Z", 1, 1, 3), ("d0", 1), ("Z", 1, 0, 3), ("F", 7), ("Z", 2, 1, 0), ("P", 3), ("F", 5),
+    ("Z", 2, 0, 1), ("P", 1), ("P", 7), ("P", 5), ("F", 6), ("Z", 2, 1, 1), ("P", 0), ("d1", -1, 0), ("d1", -1, 1),
+    ("Z", 2, 0, 2), ("P", 2), ("P", 6), ("Z", 2, 1, 2), ("P", 4), ("g", 0), ("d2",), ("Z", 3, 0, 0), ("d0", 0),
+    ("b2",), ("d1", 1, 1), ("d1", 1, 0), ("Z", 2, 1, 3), ("Z", 2, 0, 3), ("Z", 3, 1, 0), ("Z", 3, 0, 1),
+    ("Z", 3, 1, 1), ("g", 1), ("Z", 3, 0, 2), ("Z", 3, 1, 2), ("b1", 0, 0), ("b1", 0, 1), ("d1", 0, 1), ("d1", 0, 0),
+    ("Z", 3, 1, 3), ("Z", 3, 0, 3), ("d3", 1), ("g", 2), ("b3", 1), ("b3", 0), ("ZF", 0), ("ZF", 1), ("ZF", 2),
+    ("d3", 0), ("g", 3), ("ZF", 3), ("g", 4), ("H", 0), ("g", 5), ("H", 1), ("H", 2), ("AO",), ("g", 6), ("AE",),
+    ("RB",), ("RD",),
+)
 
 
 def kernel(
     x_in, c_in, up_in, down_in, g_in,
     out_hbm, dtok_hbm, gu_hbm, gd_hbm, gg_ref,
-    xo, co, ws, w_in, wz, out_ref, dtok_ref, gu_ref, gd_ref, xt, nc, w, wa, gr, gcol, inv_s, pre_s, dh_s, hd, md_s, gs, g, xr, zs, zr,
+    xo, co, ws, w_in, wz, out_ref, dtok_ref, go, xt, nc, w, wa, gr, gcol, inv_s, pre_s, dh_s, hd, md_s, gs, g, xr, zs, zr,
     br, dn, b0, b1, bq0, bq1, d0, d1, dq0, dq1, stage, ga, ggp, ggr, ggx, ggy, ggz, ggc,
     send_sem, recv_sem, copy_sem,
 ):
@@ -224,6 +240,17 @@
 
     wz[z, pl.ds(DZ + 16, 16), :] = jnp.zeros((16, FM), BF16)
     pack(wz, z, own)
+
+    def pack_parts(k, val):
+        tail = jnp.concatenate([val[:, FM:], jnp.zeros((FP - DZ, FP - FM), F32)], axis=0).T[:16]
+        for q in range(NY):
+            g[k, q, pl.ds(0, DC)] = val[q * DC:(q + 1) * DC, :FM]
+            for i in (0, 1):
+                g[k, q, pl.ds(RP - 8, 8), pl.ds(i * TB, TB)] = tail[i * 8:i * 8 + 8, q * DC:q * DC + TB]
+
+    def unpack_part(val):
+        tail = jnp.concatenate([val[RP - 8:, :TB], val[RP - 8:, TB:2 * TB], jnp.zeros((TB - 16, TB), F32)], axis=0)
+        return jnp.concatenate([val[:DC], tail.T[:DC, :16]], axis=1)
 
     def w_at(off, sub):
         o, n = SUBS[sub]
@@ -356,15 +383,18 @@
 
     core = {}
     ggr[...] = jnp.zeros_like(ggr)
-    g[:, pl.ds(DZ + 16, 16), :] = jnp.zeros((NZ, 16, FM), F32)
+    g[...] = jnp.zeros_like(g)
     ones = jnp.ones((8, FP), BF16)
 
     def fold(k):
         core[k].wait_recv()
+        total = gs[k] + xr[k].astype(F32)
+        pack_parts(k, total)
+        gs[k] = total
+
+    def gain_part(k):
         zc = pz(ZORDER[k])
-        total = gs[k] + xr[k].astype(F32)
-        pack(g, k, total)
-        v = total * w[d, rows(zc, DZ)].astype(F32)
+        v = gs[k] * w[d, rows(zc, DZ)].astype(F32)
         high = v.astype(BF16)
         low = (v - high.astype(F32)).astype(BF16)
         ggr[:, pl.ds(0, DZ)] = dot(ones, high, 1, 1) + dot(ones, low, 1, 1)
@@ -411,24 +441,44 @@
 
     zmsg = {}
 
-    def z_reduce(s, k, p):
-        for sub in (0, 1):
-            if s == 0 and sub != p:
-                continue
-            o, n = SUBS[sub]
-            r = pl.ds(o, n)
-            val = g[k, r]
-            if (p, s - 1, sub) in zmsg:
-                zmsg[p, s - 1, sub].wait_recv()
-                val = val + zr[p, s - 1, r].astype(F32)
-            zs[p, s, r] = val.astype(BF16)
-            zmsg[p, s, sub] = msg.start(zs.at[p, s, r], zr.at[p, s, r], dev("z", 1 - 2 * p))
+    def z_reduce(s, p, j):
+        k = 0 if s == 0 else 2 * s - 1 + p
+        q = py(ORDER[j])
+        val = g[k, q]
+        if (s - 1, p, j) in zmsg:
+            zmsg[s - 1, p, j].wait_recv()
+            val = val + zr[p, s - 1, q].astype(F32)
+        zs[p, s, q] = val.astype(BF16)
+        zmsg[s, p, j] = msg.start(zs.at[p, s, q], zr.at[p, s, q], dev("z", 1 - 2 * p))
+
+    back, hands = {}, {}
+
+    def z_final(j):
+        q = py(ORDER[j])
+        for p in (0, 1):
+            zmsg[3, p, j].wait_recv()
+        val = (g[7, q] + zr[0, 3, q].astype(F32) + zr[1, 3, q].astype(F32)).astype(BF16)
+        if j < 3:
+            stage[j] = val
+            back[j] = msg.start(stage.at[j], ga.at[d, y], dev("y", ORDER[j]))
+        else:
+            ga[d, y] = val
+            hands[j] = msg.start(ga.at[d, y], ga.at[d, y], dev("c"))
+
+    def hand_on(j):
+        back[j].wait_recv()
+        ref = ga.at[d, py(-ORDER[j])]
+        hands[j] = msg.start(ref, ref, dev("c"))
+
+    def assemble(i):
+        for j in range(NY):
+            go[i, :, pl.ds(j * FS, FS)] = unpack_part(ga[i, j].astype(F32)).astype(BF16)
 
     class Reduce:
         def __init__(self, ref, a, b, halves, r0, r1, q0, q1):
             self.ref, self.a, self.b, self.h = ref, a, b, halves
             self.r0, self.r1, self.q0, self.q1 = r0, r1, q0, q1
-            self.p0, self.p1 = {}, {}
+            self.p0, self.p1, self.m1 = {}, {}, {}
 
         def at(self, a, b):
             return (px(a), py(b)) if self.a == "x" else (px(b), py(a))
@@ -442,23 +492,21 @@
                 self.p0[b].append(msg.start(
                     self.ref.at[xi, yi, pl.ds(o, n)], self.r0.at[i, s, pl.ds(0, n)], dev(self.a, 1 - 2 * s)))
 
-        def send1(self, b):
+        def send1(self, b, s):
             i = ORDER.index(b)
-            self.p1[b] = []
-            for s in (0, 1):
-                o, n = self.h[s]
-                xi, yi = self.at(1 - 2 * s, b)
-                self.p0[b][s].wait_recv()
-                self.ref[xi, yi, pl.ds(o, n)] = (
-                    self.ref[xi, yi, pl.ds(o, n)].astype(F32) + self.r0[i, s, pl.ds(0, n)].astype(F32)
-                ).astype(BF16)
-                self.p1[b].append(msg.start(self.ref.at[xi, yi], self.r1.at[i, s], dev(self.a, 1 - 2 * s)))
+            o, n = self.h[s]
+            xi, yi = self.at(1 - 2 * s, b)
+            self.p0[b][s].wait_recv()
+            self.ref[xi, yi, pl.ds(o, n)] = (
+                self.ref[xi, yi, pl.ds(o, n)].astype(F32) + self.r0[i, s, pl.ds(0, n)].astype(F32)
+            ).astype(BF16)
+            self.p1[b, s] = msg.start(self.ref.at[xi, yi], self.r1.at[i, s], dev(self.a, 1 - 2 * s))
 
         def sum1(self, b):
             i = ORDER.index(b)
             xi, yi = self.at(0, b)
             for s in (0, 1):
-                self.p1[b][s].wait_recv()
+                self.p1[b, s].wait_recv()
             return self.ref[xi, yi].astype(F32) + self.r1[i, 0].astype(F32) + self.r1[i, 1].astype(F32)
 
         def second0(self):
@@ -470,20 +518,17 @@
                 self.m0.append(msg.start(
                     self.ref.at[xi, yi, pl.ds(o, n)], self.q0.at[s, pl.ds(0, n)], dev(self.b, 1 - 2 * s)))
 
-        def second1(self):
-            self.m1 = []
-            for s in (0, 1):
-                b = 1 - 2 * s
-                xi, yi = self.at(0, b)
-                o, n = self.h[s]
-                total = self.sum1(b)
-                self.m0[s].wait_recv()
-                other = slice(n, None) if o == 0 else slice(0, o)
-                self.ref[xi, yi, pl.ds(o, n)] = (
-                    total[o:o + n] + self.q0[s, pl.ds(0, n)].astype(F32)).astype(BF16)
-                so, sn = self.h[1 - s]
-                self.ref[xi, yi, pl.ds(so, sn)] = total[other].astype(BF16)
-                self.m1.append(msg.start(self.ref.at[xi, yi], self.q1.at[s], dev(self.b, b)))
+        def second1(self, s):
+            b = 1 - 2 * s
+            xi, yi = self.at(0, b)
+            o, n = self.h[s]
+            total = self.sum1(b)
+            self.m0[s].wait_recv()
+            self.ref[xi, yi, pl.ds(o, n)] = (
+                total[o:o + n] + self.q0[s, pl.ds(0, n)].astype(F32)).astype(BF16)
+            so, sn = self.h[1 - s]
+            self.ref[xi, yi, pl.ds(so, sn)] = total[so:so + sn].astype(BF16)
+            self.m1[s] = msg.start(self.ref.at[xi, yi], self.q1.at[s], dev(self.b, b))
 
         def result(self):
             total = self.sum1(0)
@@ -508,95 +553,52 @@
             dn[xi, j, pl.ds(DX, EX)] = jnp.broadcast_to(
                 md_s[:, j * TB:(j + 1) * TB], (EX, TB)).astype(BF16)
 
-    grad_chunk(0)
-    branch_block(2)
-    rb.send0(2)
-    normed_block(2)
-    for b in ORDER:
-        rd.send0(b)
-    fold(0)
-    z_reduce(0, 0, 0)
-    z_reduce(0, 0, 1)
-    grad_chunk(1)
-    grad_chunk(2)
-    branch_block(1)
-    rb.send0(1)
-    branch_block(-1)
-    rb.send0(-1)
-    fold(1)
-    fold(2)
-    branch_block(0)
-    rb.send0(0)
-    normed_block(1)
-    normed_block(-1)
-    z_reduce(1, 1, 0)
-    z_reduce(1, 2, 1)
-    rb.send1(2)
-    rd.send1(2)
-    grad_chunk(3)
-    grad_chunk(4)
-    normed_block(0)
-    for b in (1, -1, 0):
-        rb.send1(b)
-        rd.send1(b)
-    fold(3)
-    fold(4)
-    z_reduce(2, 3, 0)
-    z_reduce(2, 4, 1)
-    for k in (5, 6, 7):
-        grad_chunk(k)
-    rb.second0()
-    rd.second0()
-    for k in (5, 6, 7):
-        fold(k)
-    gain = gain_x()
-    z_reduce(3, 5, 0)
-    z_reduce(3, 6, 1)
-    gain = gain_y(gain)
-    rb.second1()
-    gain = gain_z(gain)
-    rd.second1()
-    gain = gain_ring(gain, 1)
-
-    xf = xo[...].astype(F32)
-    out_ref[...] = (xf + rb.result()).astype(BF16)
-    stores = [pltpu.make_async_copy(out_ref, out_hbm, copy_sem.at[0])]
-    stores[0].start()
-    gain = gain_ring(gain, 2)
-    total = rd.result()
-    dnorm = total[:DX]
-    inv = inv_s[...]
-    mean_dot = total[DX:DX + 1] / D
-    unit = xf * inv
-    dtok_ref[...] = (
-        co[...].astype(F32) + inv * (dnorm * gcol[x] - unit * mean_dot)
-    ).astype(BF16)
-    stores.append(pltpu.make_async_copy(dtok_ref, dtok_hbm, copy_sem.at[1]))
-    stores[1].start()
-    gain = gain_ring(gain, 3)
-
-    for p in (0, 1):
-        for sub in (0, 1):
-            zmsg[p, 3, sub].wait_recv()
-    final = g[7] + zr[0, 3].astype(F32) + zr[1, 3].astype(F32)
-    final = jnp.concatenate([final[:DZ], tail_of(final)], axis=1).astype(BF16)
-    stage[...] = dot(select, final, 0, 0).astype(BF16).reshape(NY, RP, FP)
-    back = [msg.start(stage.at[py(off)], ga.at[d, y], dev("y", off)) for off in (1, -1, 2)]
-    ga[d, y] = stage[y]
-    hands = [msg.start(ga.at[d, y], ga.at[d, y], dev("c"))]
-    gain = gain_c(gain)
-    for cp, off in zip(back, (1, -1, 2)):
-        cp.wait_recv()
-        ref = ga.at[d, py(-off)]
-        hands.append(msg.start(ref, ref, dev("c")))
-    for cp in hands:
-        cp.wait_recv()
-    for i, ref in enumerate((gu_ref, gd_ref)):
+    def out_result():
+        out_ref[...] = (xo[...].astype(F32) + rb.result()).astype(BF16)
+        stores[0].start()
+
+    def dtok_result():
+        total = rd.result()
+        dnorm = total[:DX]
+        inv = inv_s[...]
+        mean_dot = total[DX:DX + 1] / D
+        unit = xo[...].astype(F32) * inv
+        dtok_ref[...] = (
+            co[...].astype(F32) + inv * (dnorm * gcol[x] - unit * mean_dot)
+        ).astype(BF16)
+        stores[1].start()
+
+    chain = [gain_x, gain_y, gain_z, lambda m: gain_ring(m, 1), lambda m: gain_ring(m, 2),
+             lambda m: gain_ring(m, 3), gain_c]
+    gain = None
+
+    def gain_step(i):
+        nonlocal gain
+        gain = chain[i](gain) if i else chain[0]()
+
+    stores = [
+        pltpu.make_async_copy(src, dst, copy_sem.at[i])
+        for i, (src, dst) in enumerate((
+            (out_ref, out_hbm), (dtok_ref, dtok_hbm), (go.at[0], gu_hbm), (go.at[1], gd_hbm)))
+    ]
+
+    def other_core():
         for j in range(NY):
-            ref[:, pl.ds(j * FS, FS)] = ga[i, j][:DC, :FS]
-    for i, (ref, hbm) in enumerate(((gu_ref, gu_hbm), (gd_ref, gd_hbm))):
-        stores.append(pltpu.make_async_copy(ref, hbm, copy_sem.at[2 + i]))
-        stores[2 + i].start()
+            hands[j].wait_recv()
+        assemble(e)
+
+    steps = {
+        "B": branch_block, "N": normed_block, "G": grad_chunk, "F": fold, "P": gain_part,
+        "Z": z_reduce, "ZF": z_final, "H": hand_on, "AO": lambda: assemble(d), "AE": other_core,
+        "b0": rb.send0, "b1": rb.send1, "b2": rb.second0, "b3": rb.second1, "RB": out_result,
+        "d0": rd.send0, "d1": rd.send1, "d2": rd.second0, "d3": rd.second1, "RD": dtok_result,
+        "g": gain_step,
+    }
+    for name, *where in SCHEDULE:
+        steps[name](*where)
+
+    for i in (2, 3):
+        stores[i].start()
     for cp in gain:
         cp.wait_recv()
     total = jnp.where(d == 0, ggc[0], ggc[1]) * SCALE
@@ -635,8 +637,7 @@
             vm((NZ, ZP, FM)),
             vm((DX, TB)),
             vm((DX, TB)),
-            vm((DC, NY * FS)),
-            vm((DC, NY * FS)),
+            vm((2, DC, NY * FS)),
             vm((D, T)),
             vm((2, D, T)),
             vm((2, D, FP)),
@@ -649,10 +650,10 @@
             vm((2, FP, T)),
             vm((1, T), F32),
             vm((NZ, DZ, FP), F32),
-            vm((NZ, ZP, FM), F32),
+            vm((NZ, NY, RP, FM), F32),
             vm((NZ, DZ, FP)),
-            vm((2, 4, ZP, FM)),
-            vm((2, 4, ZP, FM)),
+            vm((2, 4, NY, RP, FM)),
+            vm((2, 4, NY, RP, FM)),
             vm((NX, NY, DX, TB)),
             vm((NX, NY, DE, TB)),
             vm((4, 2, 400, TB)),
@@ -663,8 +664,8 @@
             vm((4, 2, DE, TB)),
             vm((2, 416, TB)),
             vm((2, DE, TB)),
-            vm((NY, RP, FP)),
-            vm((2, NY, RP, FP)),
+            vm((3, RP, FM)),
+            vm((2, NY, RP, FM)),
             vm((NX, 8, TB), F32),
             vm((8, FP), F32),
             vm((3, 8, TB), F32),
@@ -681,13 +682,30 @@
     )(x, c, up, down, g)
 
 
+def finish(out_in, dtok_in, gu_in, gd_in, gg_in, out_ref, dtok_ref, gu_ref, gd_ref, gg_ref):
+    out_ref[...] = out_in[...]
+    dtok_ref[...] = dtok_in[...]
+    gu_ref[...] = gu_in[...].astype(F32) * SCALE
+    gd_ref[...] = gd_in[...].astype(F32) * SCALE
+    gg_ref[...] = gg_in[...]
+
+
 def on_device(tokens, gain, w_up, w_down, cotangent):
-    out, d_tokens, grad_up, grad_down, grad_gain = block(
-        tokens.T, cotangent.T, w_up, w_down.T, gain.reshape(1, DX))
-    return (
-        out.T, d_tokens.T, grad_up.astype(F32) * SCALE, grad_down.T.astype(F32) * SCALE,
-        grad_gain.reshape(DX),
-    )
+    parts = block(tokens.T, cotangent.T, w_up, w_down.T, gain.reshape(1, DX))
+    spec = pl.BlockSpec(memory_space=pltpu.VMEM)
+    out, d_tokens, grad_up, grad_down, grad_gain = pl.pallas_call(
+        finish,
+        out_shape=(
+            jax.ShapeDtypeStruct((DX, TB), BF16),
+            jax.ShapeDtypeStruct((DX, TB), BF16),
+            jax.ShapeDtypeStruct((DC, NY * FS), F32),
+            jax.ShapeDtypeStruct((DC, NY * FS), F32),
+            jax.ShapeDtypeStruct((1, DX), F32),
+        ),
+        in_specs=[spec] * 5,
+        out_specs=(spec,) * 5,
+    )(*parts)
+    return out.T, d_tokens.T, grad_up, grad_down.T, grad_gain.reshape(DX)
 
 
 def solution(mesh):

time: 127 us -> 117 us (0.921)
  Pallas kernels: 119 us -> 113 us
  other arithmetic: 2.91 us -> 0.61 us
  local copies, waits for them, and re-layouts: 3.62 us -> 1.94 us
    pallas_call x1, Pallas kernels: 119 us -> 111 us  [block(): pl.pallas_call(kernel, out_shape=(jax.ShapeDtypeStruct((DX, TB), BF16), j...]
    pallas_call x0 -> x1, Pallas kernels: none -> 2.49 us  [on_device(): pl.pallas_call(finish, out_shape=(jax.ShapeDtypeStruct((DX, TB), BF16), j...]
    mul x1 -> x0, other arithmetic: 2.31 us -> none  [on_device(): grad_down.T.astype(F32) * SCALE]
where the time goes in v3:
time: 117 us; the launch traced here: 116 us
  Pallas kernels  113 us (97%)
  local copies, waits for them, and re-layouts  1.94 us (2%)
    pallas_call x1, Pallas kernels, block(): pl.pallas_call(kernel, out_shape=(jax.ShapeDtypeStruct((DX, TB), BF16), j...  111 us
    pallas_call x1, Pallas kernels, on_device(): pl.pallas_call(finish, out_shape=(jax.ShapeDtypeStruct((DX, TB), BF16), j...  2.49 us

profile of v3, /device:TPU:1, one launch (start us, length us, event | category | flops | bytes accessed | tf_op | source)
XLA Modules:
  0.0 116.4 jit_solution(12578753200042820486)
XLA Ops:
  0.6 0.0 copy-start.1
  0.6 0.7 copy-done.1
  1.3 0.6 reshape.16.g_in
  1.9 110.7 %shard_map.92 = (bf16[800,128]{1,0:T(8,128)(2,1)}, bf16[800,128]{1,0:T(8,128)(2,1)}, bf16[100,1600]{1,0:T(8,128)(2,1)}, bf16[100,1600]{1,0:T(8,128)(2,1)}, f32[1,800]{1,0:T(1,128)}) custom-call(bf16[800,128]{1,0:T(8,128)(2,1)} %bitcast.7, bf16[800,128]{1,0:T(8,128)(2,1)} %bitcast.8, bf16[100,1600]{1,0:T(8,128)(2,1)} %up_in.1, bf16[100,1600]{1,0:T(8,128)(2,1)} %bitcast.6, ...), custom_call_target="tpu_custom_call" | custom-call | tf_op jit(solution)/shard_map/pallas_call | solution.py:621
  112.6 2.5 %shard_map.93 = (bf16[800,128]{1,0:T(8,128)(2,1)}, bf16[800,128]{1,0:T(8,128)(2,1)}, f32[100,1600]{1,0:T(8,128)}, f32[100,1600]{1,0:T(8,128)}, f32[1,800]{1,0:T(1,128)}) custom-call(bf16[800,128]{1,0:T(8,128)(2,1)} %get-tuple-element.15.out_in, bf16[800,128]{1,0:T(8,128)(2,1)} %get-tuple-element.16.dtok_in, bf16[100,1600]{1,0:T(8,128)(2,1)} %get-tuple-element.17.gu_in, ...), custom_call_target="tpu_custom_call" | custom-call | tf_op jit(solution)/shard_map/pallas_call | solution.py:696
  115.1 0.0 copy-start
  115.1 0.7 copy-done
  115.8 0.6 reduce
Async XLA Ops:
  0.6 0.7 copy-start.1
  115.1 0.7 copy-start

commit v4 on v3

--- a/solution.py
+++ b/solution.py
@@ -24,8 +24,6 @@
 EX = 16
 DE = DX + EX
 FM = 384
-ZP = 432
-SUBS = ((0, 208), (208, 224))
 HALF = ((0, 400), (400, 400))
 HALFE = ((0, 400), (400, 416))
 ORDER = (2, 1, -1, 0)
@@ -71,6 +69,19 @@
 
 
 N_MESSAGES = 224
+
+GATHER = (
+    ("wa",), ("xm",), ("cm",), ("wz", 3), ("xn", 0), ("cn", 0), ("gs",), ("wr",), ("wz", 1), ("wf", 0, 0, 3),
+    ("wf", 0, 1, 3), ("wz", 2), ("xf", 0), ("xf", 1), ("xn", 1), ("xn", -1), ("wf", 0, 0, 1), ("wf", 0, 1, 1),
+    ("cf", 0), ("cf", 1), ("cn", 1), ("wf", 1, 1, 3), ("cn", -1), ("wf", 1, 0, 3), ("cg", 0, 0), ("cg", 0, 1),
+    ("wf", 0, 0, 2), ("wf", 0, 1, 2), ("wf", 1, 0, 1), ("wf", 1, 1, 1), ("xn", 2), ("nm", 0), ("xg", 0, 0),
+    ("xg", 0, 1), ("wz", 0), ("wu", 0), ("wf", 2, 1, 3), ("wf", 1, 0, 2), ("wf", 1, 1, 2), ("cg", 1, 0), ("cg", 1, 1),
+    ("wf", 2, 1, 1), ("xg", 1, 0), ("xg", 1, 1), ("wf", 0, 0, 0), ("wf", 0, 1, 0), ("wu", -1), ("wu", 1),
+    ("cg", -1, 0), ("cg", -1, 1), ("wf", 2, 0, 2), ("xg", -1, 0), ("xg", -1, 1), ("wf", 1, 0, 0), ("wu", -2),
+    ("cn", 2), ("wf", 1, 1, 0), ("wf", 2, 0, 0), ("wu", 2), ("wu", -3), ("xg", 2, 0), ("xg", 2, 1), ("nm", -1),
+    ("nm", 1), ("wu", 3), ("wu", 4), ("cg", 2, 0), ("cg", 2, 1), ("ww",), ("db", 0), ("db", -1), ("db", 1), ("db", 2),
+    ("nm", 2), ("pc",), ("gl",), ("hp",),
+)
 
 SCHEDULE = (
     ("B", 2), ("N", 2), ("G", 0), ("b0", 2), ("N", 1), ("B", 1), ("b0", 1), ("B", -1), ("N", -1), ("b0", -1),
@@ -92,7 +103,7 @@
 def kernel(
     x_in, c_in, up_in, down_in, g_in,
     out_hbm, dtok_hbm, gu_hbm, gd_hbm, gg_ref,
-    xo, co, ws, w_in, wz, out_ref, dtok_ref, go, xt, nc, w, wa, gr, gcol, inv_s, pre_s, dh_s, hd, md_s, gs, g, xr, zs, zr,
+    xo, co, ws, w_in, wz, out_ref, dtok_ref, go, xt, nc, w, relay, gr, gcol, inv_s, pre_s, dh_s, slope, hd, md_s, gs, g, xr, zs, zr,
     br, dn, b0, b1, bq0, bq1, d0, d1, dq0, dq1, stage, ga, ggp, ggr, ggx, ggy, ggz, ggc,
     send_sem, recv_sem, copy_sem,
 ):
@@ -154,12 +165,18 @@
 
     w_in[...] = jnp.zeros_like(w_in)
     for j in range(NY):
-        w_in[j, pl.ds(0, DC), pl.ds(0, FS)] = ws[:, j * FS:(j + 1) * FS]
+        w_in[j, pl.ds(0, DC)] = ws[:, j * FS:j * FS + FM]
+        tail = jnp.concatenate([ws[:, j * FS + FM:(j + 1) * FS].astype(F32), jnp.zeros((DC, TB - 16), F32)], axis=1)
+        tail = jnp.concatenate([tail, jnp.zeros((TB - DC, TB), F32)], axis=0).T
+        w_in[j, pl.ds(RP - 16, 16), pl.ds(0, 2 * TB)] = jnp.concatenate([
+            jnp.concatenate([ws[RP - 16:DC, j * FS:j * FS + 2 * TB].astype(F32),
+                             jnp.zeros((RP - 8 - DC, 2 * TB), F32)], axis=0),
+            jnp.concatenate([tail[:8], tail[8:16]], axis=1)], axis=0).astype(BF16)
     for cp in loads:
         cp.wait()
     xt[rows(x, DX), lanes(y)] = xo[...]
     nc[1, rows(x, DX), lanes(y)] = co[...]
-    gain_own = g_in[...].astype(F32)
+    gain_own = g_in[...].astype(F32).reshape(1, DX)
     gr[x] = jnp.zeros_like(gr[0])
     gr[x, :, pl.ds(0, DX)] = jnp.broadcast_to(gain_own, (8, DX))
     pl.semaphore_wait(barrier, len(partners))
@@ -167,7 +184,7 @@
     class Gather:
         def __init__(self, ref, first, second):
             self.ref, self.a, self.b = ref, first, second
-            self.n1, self.n2 = {}, {}
+            self.n1, self.n2, self.m2 = {}, {}, {}
 
         def at(self, a, b, half=None):
             xi, yi = (px(a), py(b)) if self.a == "x" else (px(b), py(a))
@@ -184,62 +201,32 @@
         def second(self, a):
             self.n1[a] = [self.go(a, 0, self.b, 1), self.go(a, 0, self.b, -1)]
 
-        def first_forward(self):
-            self.m1[0].wait_recv()
-            m2p = self.go(-1, 0, self.a, 1, 0)
-            self.m1[1].wait_recv()
-            m2m = self.go(1, 0, self.a, -1, 1)
-            self.m2 = [m2p, m2m]
+        def first_forward(self, s):
+            self.m1[s].wait_recv()
+            self.m2[s] = self.go(2 * s - 1, 0, self.a, 1 - 2 * s, s)
 
         def first_done(self):
-            for cp in self.m2:
-                cp.wait_recv()
-
-        def second_forward(self, a):
-            self.n1[a][0].wait_recv()
-            p = self.go(a, -1, self.b, 1, 0)
-            self.n1[a][1].wait_recv()
-            m = self.go(a, 1, self.b, -1, 1)
-            self.n2[a] = [p, m]
-
-        def second_done(self, a):
-            for cp in self.n2[a]:
-                cp.wait_recv()
+            while self.m2:
+                self.m2.popitem()[1].wait_recv()
+
+        def second_step(self, a):
+            if a == 2:
+                self.first_done()
+            self.second(a)
+
+        def second_forward(self, a, s):
+            self.n1[a][s].wait_recv()
+            self.n2[a, s] = self.go(a, 2 * s - 1, self.b, 1 - 2 * s, s)
+
+        def second_done(self):
+            for a in ORDER:
+                for s in (0, 1):
+                    self.n2[a, s].wait_recv()
 
     gx = Gather(lambda r, l: xt.at[r, l], "x", "y")
     gc = Gather(lambda r, l: nc.at[1, r, l], "y", "x")
 
     gain_msgs = [msg.start(gr.at[x], gr.at[x], dev("x", off)) for off in (1, -1, 2)]
-    a2a = [msg.start(w_in.at[py(off)], wa.at[y], dev("y", off)) for off in (1, -1, 2)]
-    gx.first()
-    gc.first()
-    gx.second(0)
-    gc.second(0)
-    wa[y] = w_in[y]
-
-    r_i = lax.broadcasted_iota(jnp.int32, (DZ, NY * RP), 0)
-    c_i = lax.broadcasted_iota(jnp.int32, (DZ, NY * RP), 1)
-    shift = jnp.where(r_i >= 3 * DC, 3, jnp.where(r_i >= 2 * DC, 2, jnp.where(r_i >= DC, 1, 0)))
-    select = jnp.where(c_i == r_i + (RP - DC) * shift, 1.0, 0.0).astype(BF16)
-
-    for cp in a2a:
-        cp.wait_recv()
-    own = dot(select, wa[...].reshape(NY * RP, FP), 1, 0)
-    w[d, rows(z, DZ)] = own.astype(BF16)
-
-    def pack(ref, i, val):
-        tail = jnp.concatenate([val[:, FM:], jnp.zeros((FP - DZ, FP - FM), F32)], axis=0).T[:16]
-        ref[i, pl.ds(0, DZ)] = val[:, :FM].astype(ref.dtype)
-        ref[i, pl.ds(DZ, 16)] = tail[:, :FM].astype(ref.dtype)
-        ref[i, pl.ds(DZ + 16, 16), pl.ds(0, FP - FM)] = tail[:, FM:].astype(ref.dtype)
-
-    def tail_of(val):
-        tail = jnp.concatenate([val[DZ:DZ + 16], val[DZ + 16:, :FP - FM]], axis=1)
-        tail = jnp.concatenate([tail, jnp.zeros((FP - FM - 16, FP), F32)], axis=0)
-        return tail.T[:DZ]
-
-    wz[z, pl.ds(DZ + 16, 16), :] = jnp.zeros((16, FM), BF16)
-    pack(wz, z, own)
 
     def pack_parts(k, val):
         tail = jnp.concatenate([val[:, FM:], jnp.zeros((FP - DZ, FP - FM), F32)], axis=0).T[:16]
@@ -250,67 +237,66 @@
 
     def unpack_part(val):
         tail = jnp.concatenate([val[RP - 8:, :TB], val[RP - 8:, TB:2 * TB], jnp.zeros((TB - 16, TB), F32)], axis=0)
-        return jnp.concatenate([val[:DC], tail.T[:DC, :16]], axis=1)
-
-    def w_at(off, sub):
-        o, n = SUBS[sub]
-        return wz.at[pz(off), pl.ds(o, n)]
-
-    def hand(off):
-        ref = w.at[d, rows(pz(off), DZ)]
-        wc.append(msg.start(ref, ref, dev("c")))
-
-    def unpack(off):
-        r = rows(pz(off), DZ)
-        w[d, r, pl.ds(0, FM)] = wz[pz(off), pl.ds(0, DZ)]
-        w[d, r, pl.ds(FM, FP - FM)] = tail_of(wz[pz(off)].astype(F32)).astype(BF16)
-        hand(off)
-
-    zp, zm, wc = {}, {}, []
-
-    def z_send(s):
-        for sub in (0, 1):
-            if s < 3 or sub == 0:
-                zp[s, sub] = msg.start(w_at(-s, sub), w_at(-s, sub), dev("z", 1))
-            if s < 3 or sub == 1:
-                zm[s, sub] = msg.start(w_at(s, sub), w_at(s, sub), dev("z", -1))
-
-    def z_step(s):
-        for sub in (0, 1):
-            if (s, sub) in zp:
-                zp[s, sub].wait_recv()
-                if s < 2 or (s == 2 and sub == 0):
-                    ref = w_at(-(s + 1), sub)
-                    zp[s + 1, sub] = msg.start(ref, ref, dev("z", 1))
-            if (s, sub) in zm:
-                zm[s, sub].wait_recv()
-                if s < 2 or (s == 2 and sub == 1):
-                    ref = w_at(s + 1, sub)
-                    zm[s + 1, sub] = msg.start(ref, ref, dev("z", -1))
-        unpack(s + 1)
-        if s < 3:
-            unpack(-(s + 1))
-
-    z_send(0)
-    hand(0)
-
-    gx.first_forward()
-    gc.first_forward()
-    for a in (-1, 1):
-        gx.second(a)
-        gc.second(a)
-    for cp in gain_msgs:
-        cp.wait_recv()
+        return jnp.concatenate([val[:DC], tail.T[:DC]], axis=1)
+
+    a2a, zw, wc = {}, {}, {}
+    late = {0: (0, 2), 1: (1, 3)}
+
+    def w_at(off, j):
+        return wz.at[pz(off), py(ORDER[j])]
+
+    def w_apart():
+        a2a[0] = msg.start(w_in.at[py(2)], relay, dev("y", 1 - 2 * d))
+        for i in (1, 2):
+            a2a[i] = msg.start(w_in.at[py(ORDER[i])], wz.at[z, y], dev("y", ORDER[i]))
+        wz[z, y] = w_in[y]
+
+    def w_relay():
+        a2a[0].wait_recv()
+        a2a[0] = msg.start(relay, wz.at[z, py(2 * d - 1)], dev("y", 1 - 2 * d))
+
+    def w_first(j):
+        if j < 3:
+            a2a[(0, 2, 1)[j]].wait_recv()
+        for p in (0, 1):
+            zw[0, p, j] = msg.start(w_at(0, j), w_at(0, j), dev("z", 1 - 2 * p))
+
+    def w_forward(s, p, j):
+        zw[s, p, j].wait_recv()
+        ref = w_at((2 * p - 1) * (s + 1), j)
+        zw[s + 1, p, j] = msg.start(ref, ref, dev("z", 1 - 2 * p))
+
+    def w_unpack(off):
+        s = abs(off) - 1
+        for p in (0, 1):
+            for j in range(NY):
+                if (s == 3 and j in late[p]) or (s == 2 and off == (2 * p - 1) * 3 and j not in late[p]):
+                    zw[s, p, j].wait_recv()
+        zc = pz(off)
+        r = rows(zc, DZ)
+        w[d, r] = jnp.concatenate([unpack_part(wz[zc, q].astype(F32)) for q in range(NY)], axis=0).astype(BF16)
+        wc[off] = msg.start(w.at[d, r], w.at[d, r], dev("c"))
+
+    def w_done():
+        for cp in wc.values():
+            cp.wait_recv()
 
     def spread_gain(i, carry):
         column = gr[i].T[:DX, 0:1]
         gcol[i] = jnp.broadcast_to(column, (DX, TB))
         return carry
 
-    lax.fori_loop(0, NX, spread_gain, 0)
+    def all_gain():
+        for cp in gain_msgs:
+            cp.wait_recv()
+        lax.fori_loop(0, NX, spread_gain, 0)
 
     def normalise(off):
         yi = py(off)
+        if off == 0:
+            gx.first_done()
+        if off == 2:
+            gx.second_done()
 
         def square(i, acc):
             v = xt[pl.ds(pl.multiple_of(i * 160, 16), 160), lanes(yi)].astype(F32)
@@ -330,56 +316,56 @@
 
         lax.fori_loop(0, D // 160, scale, 0)
 
-    gx.first_done()
-    gx.second(2)
-    gc.first_done()
-    gc.second(2)
-    normalise(0)
-    gx.second_forward(0)
-    gc.second_forward(0)
-    z_step(0)
-    for a in (-1, 1):
-        gx.second_forward(a)
-        gc.second_forward(a)
-    z_step(1)
-    gx.second_forward(2)
-    gc.second_forward(2)
-    normalise(1)
-    normalise(-1)
-    z_step(2)
-    for a in (0, -1, 1, 2):
-        gx.second_done(a)
-    normalise(2)
-    for a in (0, -1, 1, 2):
-        gc.second_done(a)
-    z_step(3)
-    for cp in wc:
-        cp.wait_recv()
-    msg.drain()
-
-    pre_s[...] = jnp.zeros_like(pre_s)
-    dh_s[...] = jnp.zeros_like(dh_s)
-
-    def up(i, carry):
-        r = rows(i, DZ)
-        pre_s[...] += dot(w[0, r], nc[0, r], 0, 0)
+    def pre_all():
+        pre_s[...] = jnp.zeros_like(pre_s)
+
+        def body(i, carry):
+            r = rows(i, 2 * DZ)
+            pre_s[...] += dot(w[0, r], nc[0, r], 0, 0)
+            return carry
+
+        lax.fori_loop(0, NZ // 2, body, 0)
+
+    def activate():
+        def body(i, carry):
+            r = pl.ds(pl.multiple_of(i * 16, 16), 16)
+            pre = pre_s[r]
+            hd[1, r] = gelu_value(pre).astype(BF16)
+            slope[r] = gelu_slope(pre)
+            return carry
+
+        lax.fori_loop(0, FS // 16, body, 0)
+
+    def d_hidden_rows(a):
+        if a == 0:
+            gc.first_done()
+            dh_s[...] = jnp.zeros_like(dh_s)
+        if a == 2:
+            gc.second_done()
+        r = rows(px(a), DX)
         dh_s[...] += dot(w[1, r], nc[1, r], 0, 0)
-        return carry
-
-    lax.fori_loop(0, NZ, up, 0)
+
+    def d_pre():
+        def body(i, acc):
+            r = pl.ds(pl.multiple_of(i * 16, 16), 16)
+            dpre = dh_s[r] * slope[r]
+            hd[0, r] = dpre.astype(BF16)
+            return acc + jnp.sum(dpre * pre_s[r], axis=0, keepdims=True)
+
+        md_s[...] = lax.fori_loop(0, FS // 16, body, jnp.zeros((1, T), F32))
 
     hd[0, pl.ds(FS, FP - FS)] = jnp.zeros((FP - FS, T), BF16)
     hd[1, pl.ds(FS, FP - FS)] = jnp.zeros((FP - FS, T), BF16)
-
-    def act(i, acc):
-        r = pl.ds(pl.multiple_of(i * 16, 16), 16)
-        pre = pre_s[r]
-        dpre = dh_s[r] * gelu_slope(pre)
-        hd[1, r] = gelu_value(pre).astype(BF16)
-        hd[0, r] = dpre.astype(BF16)
-        return acc + jnp.sum(dpre * pre, axis=0, keepdims=True)
-
-    md_s[...] = lax.fori_loop(0, FS // 16, act, jnp.zeros((1, T), F32))
+    steps = {
+        "xm": gx.first, "xf": gx.first_forward, "xn": gx.second_step, "xg": gx.second_forward,
+        "cm": gc.first, "cf": gc.first_forward, "cn": gc.second_step, "cg": gc.second_forward,
+        "wa": w_apart, "wr": w_relay, "wz": w_first, "wf": w_forward, "wu": w_unpack, "ww": w_done,
+        "gs": all_gain, "nm": normalise, "pc": pre_all, "gl": activate, "db": d_hidden_rows,
+        "hp": d_pre,
+    }
+    for name, *where in GATHER:
+        steps[name](*where)
+    msg.drain()
 
     core = {}
     ggr[...] = jnp.zeros_like(ggr)
@@ -472,7 +458,7 @@
 
     def assemble(i):
         for j in range(NY):
-            go[i, :, pl.ds(j * FS, FS)] = unpack_part(ga[i, j].astype(F32)).astype(BF16)
+            go[i, :, pl.ds(j * FS, FS)] = unpack_part(ga[i, j].astype(F32))[:, :FS].astype(BF16)
 
     class Reduce:
         def __init__(self, ref, a, b, halves, r0, r1, q0, q1):
@@ -606,6 +592,7 @@
         row = jnp.concatenate([total[4 * i + j:4 * i + j + 1] for j in range(4)], axis=1)
         gg_ref[:, pl.ds(i * DZ, DZ)] = row[:, :DZ]
     gg_ref[...] = gg_ref[...] / gain_own
+    assert msg.n <= N_MESSAGES
     msg.drain()
     for cp in stores:
         cp.wait()
@@ -633,20 +620,21 @@
             vm((DX, TB)),
             vm((DX, TB)),
             vm((DC, NY * FS)),
-            vm((NY, RP, FP)),
-            vm((NZ, ZP, FM)),
+            vm((NY, RP, FM)),
+            vm((NZ, NY, RP, FM)),
             vm((DX, TB)),
             vm((DX, TB)),
             vm((2, DC, NY * FS)),
             vm((D, T)),
             vm((2, D, T)),
             vm((2, D, FP)),
-            vm((NY, RP, FP)),
+            vm((RP, FM)),
             vm((NX, 8, 896), F32),
             vm((NX, DX, TB), F32),
             vm((1, TB), F32),
             vm((FP, T), F32),
             vm((FP, T), F32),
+            vm((FS, T), F32),
             vm((2, FP, T)),
             vm((1, T), F32),
             vm((NZ, DZ, FP), F32),
@@ -687,11 +675,11 @@
     dtok_ref[...] = dtok_in[...]
     gu_ref[...] = gu_in[...].astype(F32) * SCALE
     gd_ref[...] = gd_in[...].astype(F32) * SCALE
-    gg_ref[...] = gg_in[...]
+    gg_ref[...] = gg_in[...].reshape(DX)
 
 
 def on_device(tokens, gain, w_up, w_down, cotangent):
-    parts = block(tokens.T, cotangent.T, w_up, w_down.T, gain.reshape(1, DX))
+    parts = block(tokens.T, cotangent.T, w_up, w_down.T, gain)
     spec = pl.BlockSpec(memory_space=pltpu.VMEM)
     out, d_tokens, grad_up, grad_down, grad_gain = pl.pallas_call(
         finish,
@@ -700,12 +688,12 @@
             jax.ShapeDtypeStruct((DX, TB), BF16),
             jax.ShapeDtypeStruct((DC, NY * FS), F32),
             jax.ShapeDtypeStruct((DC, NY * FS), F32),
-            jax.ShapeDtypeStruct((1, DX), F32),
+            jax.ShapeDtypeStruct((DX,), F32),
         ),
         in_specs=[spec] * 5,
         out_specs=(spec,) * 5,
     )(*parts)
-    return out.T, d_tokens.T, grad_up, grad_down.T, grad_gain.reshape(DX)
+    return out.T, d_tokens.T, grad_up, grad_down.T, grad_gain
 
 
 def solution(mesh):

time: 117 us -> 110 us (0.940)
  Pallas kernels: 113 us -> 109 us
  local copies, waits for them, and re-layouts: 1.94 us -> 0 us
    pallas_call x1, Pallas kernels: 111 us -> 107 us  [block(): pl.pallas_call(kernel, out_shape=(jax.ShapeDtypeStruct((DX, TB), BF16), j...]
    unnamed x4 -> x0, local copies, waits for them, and re-layouts: 1.36 us -> none
where the time goes in v4:
time: 110 us
  Pallas kernels  109 us (99%)
    pallas_call x1, Pallas kernels, block(): pl.pallas_call(kernel, out_shape=(jax.ShapeDtypeStruct((DX, TB), BF16), j...  107 us
    pallas_call x1, Pallas kernels, on_device(): pl.pallas_call(finish, out_shape=(jax.ShapeDtypeStruct((DX, TB), BF16), j...  2.49 us

profile of v4, /device:TPU:1, one launch (start us, length us, event | category | flops | bytes accessed | tf_op | source)
XLA Modules:
  0.0 109.9 jit_solution(412086488848568897)
XLA Ops:
  0.6 106.8 %shard_map.92 = (bf16[800,128]{1,0:T(8,128)(2,1)}, bf16[800,128]{1,0:T(8,128)(2,1)}, bf16[100,1600]{1,0:T(8,128)(2,1)}, bf16[100,1600]{1,0:T(8,128)(2,1)}, f32[1,800]{1,0:T(1,128)}) custom-call(bf16[800,128]{1,0:T(8,128)(2,1)} %bitcast.7, bf16[800,128]{1,0:T(8,128)(2,1)} %bitcast.8, bf16[100,1600]{1,0:T(8,128)(2,1)} %up_in.1, bf16[100,1600]{1,0:T(8,128)(2,1)} %bitcast.6, ...), custom_call_target="tpu_custom_call" | custom-call | tf_op jit(solution)/shard_map/pallas_call | solution.py:608
  107.4 2.5 %shard_map.93 = (bf16[800,128]{1,0:T(8,128)(2,1)}, bf16[800,128]{1,0:T(8,128)(2,1)}, f32[100,1600]{1,0:T(8,128)}, f32[100,1600]{1,0:T(8,128)}, f32[800]{0:T(1024)}) custom-call(bf16[800,128]{1,0:T(8,128)(2,1)} %get-tuple-element.15.out_in, bf16[800,128]{1,0:T(8,128)(2,1)} %get-tuple-element.16.dtok_in, bf16[100,1600]{1,0:T(8,128)(2,1)} %get-tuple-element.17.gu_in, ...), custom_call_target="tpu_custom_call" | custom-call | tf_op jit(solution)/shard_map/pallas_call | solution.py:684

commit v5 on v4

--- a/solution.py
+++ b/solution.py
@@ -47,28 +47,36 @@
     )
 
 
+class Message:
+    def __init__(self, copy, pool, i):
+        self.copy, self.pool, self.i = copy, pool, i
+
+    def wait_recv(self):
+        self.copy.wait_recv()
+        self.copy.wait_send()
+        self.pool.append(self.i)
+
+
 class Messages:
     def __init__(self, send, recv):
-        self.send, self.recv, self.n, self.live = send, recv, 0, []
+        self.send, self.recv, self.n, self.n_send, self.pool = send, recv, 0, 0, []
 
     def start(self, src, dst, device):
-        i = self.n
-        self.n += 1
+        if self.pool:
+            i = self.pool.pop(0)
+        else:
+            i = self.n_send
+            self.n_send += 1
         cp = pltpu.make_async_remote_copy(
-            src_ref=src, dst_ref=dst, send_sem=self.send.at[i], recv_sem=self.recv.at[i],
+            src_ref=src, dst_ref=dst, send_sem=self.send.at[i], recv_sem=self.recv.at[self.n],
             device_id=device, device_id_type=MESH,
         )
+        self.n += 1
         cp.start()
-        self.live.append(cp)
-        return cp
-
-    def drain(self):
-        for cp in self.live:
-            cp.wait_send()
-        self.live = []
-
-
-N_MESSAGES = 224
+        return Message(cp, self.pool, i)
+
+
+N_MESSAGES, N_SEND = 180, 29
 
 GATHER = (
     ("wa",), ("xm",), ("cm",), ("wz", 3), ("xn", 0), ("cn", 0), ("gs",), ("wr",), ("wz", 1), ("wf", 0, 0, 3),
@@ -365,7 +373,6 @@
     }
     for name, *where in GATHER:
         steps[name](*where)
-    msg.drain()
 
     core = {}
     ggr[...] = jnp.zeros_like(ggr)
@@ -592,8 +599,7 @@
         row = jnp.concatenate([total[4 * i + j:4 * i + j + 1] for j in range(4)], axis=1)
         gg_ref[:, pl.ds(i * DZ, DZ)] = row[:, :DZ]
     gg_ref[...] = gg_ref[...] / gain_own
-    assert msg.n <= N_MESSAGES
-    msg.drain()
+    assert (msg.n, msg.n_send, len(msg.pool)) == (N_MESSAGES, N_SEND, N_SEND)
     for cp in stores:
         cp.wait()
 
@@ -660,7 +666,7 @@
             vm((4, 8, TB), F32),
             vm((NZ, 8, TB), F32),
             vm((2, 8, TB), F32),
-            pltpu.SemaphoreType.DMA((N_MESSAGES,)),
+            pltpu.SemaphoreType.DMA((N_SEND,)),
             pltpu.SemaphoreType.DMA((N_MESSAGES,)),
             pltpu.SemaphoreType.DMA((4,)),
         ],

time: 110 us -> 108 us (0.982)
  Pallas kernels: 109 us -> 107 us
    pallas_call x1, Pallas kernels: 107 us -> 104 us  [block(): pl.pallas_call(kernel, out_shape=(jax.ShapeDtypeStruct((DX, TB), BF16), j...]
where the time goes in v5:
time: 108 us
  Pallas kernels  107 us (99%)
    pallas_call x1, Pallas kernels, block(): pl.pallas_call(kernel, out_shape=(jax.ShapeDtypeStruct((DX, TB), BF16), j...  104 us
    pallas_call x1, Pallas kernels, on_device(): pl.pallas_call(finish, out_shape=(jax.ShapeDtypeStruct((DX, TB), BF16), j...  2.49 us

profile of v5, /device:TPU:1, one launch (start us, length us, event | category | flops | bytes accessed | tf_op | source)
XLA Modules:
  0.0 107.6 jit_solution(12654998861511674886)
XLA Ops:
  0.6 104.5 %shard_map.92 = (bf16[800,128]{1,0:T(8,128)(2,1)}, bf16[800,128]{1,0:T(8,128)(2,1)}, bf16[100,1600]{1,0:T(8,128)(2,1)}, bf16[100,1600]{1,0:T(8,128)(2,1)}, f32[1,800]{1,0:T(1,128)}) custom-call(bf16[800,128]{1,0:T(8,128)(2,1)} %bitcast.7, bf16[800,128]{1,0:T(8,128)(2,1)} %bitcast.8, bf16[100,1600]{1,0:T(8,128)(2,1)} %up_in.1, bf16[100,1600]{1,0:T(8,128)(2,1)} %bitcast.6, ...), custom_call_target="tpu_custom_call" | custom-call | tf_op jit(solution)/shard_map/pallas_call | solution.py:614
  105.1 2.5 %shard_map.93 = (bf16[800,128]{1,0:T(8,128)(2,1)}, bf16[800,128]{1,0:T(8,128)(2,1)}, f32[100,1600]{1,0:T(8,128)}, f32[100,1600]{1,0:T(8,128)}, f32[800]{0:T(1024)}) custom-call(bf16[800,128]{1,0:T(8,128)(2,1)} %get-tuple-element.15.out_in, bf16[800,128]{1,0:T(8,128)(2,1)} %get-tuple-element.16.dtok_in, bf16[100,1600]{1,0:T(8,128)(2,1)} %get-tuple-element.17.gu_in, ...), custom_call_target="tpu_custom_call" | custom-call | tf_op jit(solution)/shard_map/pallas_call | solution.py:690

commit v6 on v5

--- a/solution.py
+++ b/solution.py
@@ -92,26 +92,26 @@
 )
 
 SCHEDULE = (
-    ("B", 2), ("N", 2), ("G", 0), ("b0", 2), ("N", 1), ("B", 1), ("b0", 1), ("B", -1), ("N", -1), ("b0", -1),
-    ("d0", 2), ("G", 1), ("F", 0), ("Z", 0, 0, 0), ("Z", 0, 1, 1), ("Z", 0, 0, 2), ("G", 2), ("b1", 2, 0),
-    ("b1", 2, 1), ("B", 0), ("G", 3), ("G", 4), ("b1", 1, 1), ("d1", 2, 0), ("d1", 2, 1), ("Z", 0, 1, 3), ("F", 1),
-    ("F", 2), ("Z", 1, 1, 0), ("Z", 1, 0, 0), ("Z", 1, 1, 1), ("Z", 1, 0, 1), ("G", 7), ("b1", -1, 1), ("b1", -1, 0),
-    ("G", 5), ("Z", 1, 0, 2), ("b1", 1, 0), ("Z", 1, 1, 2), ("d0", -1), ("F", 3), ("b0", 0), ("N", 0), ("G", 6),
-    ("Z", 2, 0, 0), ("F", 4), ("Z", 1, 1, 3), ("d0", 1), ("Z", 1, 0, 3), ("F", 7), ("Z", 2, 1, 0), ("P", 3), ("F", 5),
-    ("Z", 2, 0, 1), ("P", 1), ("P", 7), ("P", 5), ("F", 6), ("Z", 2, 1, 1), ("P", 0), ("d1", -1, 0), ("d1", -1, 1),
-    ("Z", 2, 0, 2), ("P", 2), ("P", 6), ("Z", 2, 1, 2), ("P", 4), ("g", 0), ("d2",), ("Z", 3, 0, 0), ("d0", 0),
-    ("b2",), ("d1", 1, 1), ("d1", 1, 0), ("Z", 2, 1, 3), ("Z", 2, 0, 3), ("Z", 3, 1, 0), ("Z", 3, 0, 1),
-    ("Z", 3, 1, 1), ("g", 1), ("Z", 3, 0, 2), ("Z", 3, 1, 2), ("b1", 0, 0), ("b1", 0, 1), ("d1", 0, 1), ("d1", 0, 0),
-    ("Z", 3, 1, 3), ("Z", 3, 0, 3), ("d3", 1), ("g", 2), ("b3", 1), ("b3", 0), ("ZF", 0), ("ZF", 1), ("ZF", 2),
-    ("d3", 0), ("g", 3), ("ZF", 3), ("g", 4), ("H", 0), ("g", 5), ("H", 1), ("H", 2), ("AO",), ("g", 6), ("AE",),
-    ("RB",), ("RD",),
+    ("G", 0), ("B", 2), ("b0", 2), ("N", 2), ("d0", 2), ("G", 1), ("B", 1), ("B", -1), ("G", 2), ("b0", -1), ("G", 7),
+    ("F", 0), ("Z", 0, 0, 0), ("Z", 0, 1, 1), ("Z", 0, 0, 2), ("G", 5), ("G", 6), ("b1", 2, 1), ("b1", 2, 0),
+    ("F", 1), ("Z", 1, 0, 1), ("b0", 1), ("d0", -1), ("G", 4), ("N", 1), ("F", 2), ("Z", 1, 1, 0), ("Z", 1, 1, 2),
+    ("G", 3), ("b1", -1, 1), ("F", 7), ("Z", 1, 0, 0), ("Z", 1, 1, 1), ("d0", 1), ("b1", -1, 0), ("N", -1), ("F", 5),
+    ("Z", 0, 1, 3), ("B", 0), ("Z", 1, 0, 2), ("F", 6), ("P", 6), ("d1", 2, 0), ("P", 2), ("P", 0), ("F", 4),
+    ("Z", 2, 1, 0), ("P", 4), ("P", 5), ("P", 1), ("b2",), ("F", 3), ("P", 3), ("Z", 2, 0, 1), ("P", 7), ("g", 0),
+    ("Z", 2, 1, 2), ("Z", 1, 0, 3), ("Z", 2, 0, 0), ("d1", 2, 1), ("d0", 0), ("N", 0), ("b1", 1, 0), ("b1", 1, 1),
+    ("b0", 0), ("d1", -1, 1), ("d1", 1, 1), ("Z", 2, 1, 1), ("d1", 1, 0), ("d1", -1, 0), ("Z", 2, 0, 2),
+    ("Z", 1, 1, 3), ("Z", 3, 0, 1), ("b3", 1), ("Z", 3, 1, 0), ("Z", 2, 0, 3), ("g", 1), ("Z", 3, 1, 2),
+    ("Z", 3, 0, 0), ("d2",), ("d1", 0, 0), ("Z", 3, 1, 1), ("Z", 3, 0, 2), ("b3", 0), ("d1", 0, 1), ("Z", 2, 1, 3),
+    ("b1", 0, 1), ("b1", 0, 0), ("g", 2), ("Z", 3, 0, 3), ("ZF", 0), ("ZF", 1), ("ZF", 2), ("g", 3), ("d3", 1),
+    ("Z", 3, 1, 3), ("d3", 0), ("g", 4), ("H", 2), ("H", 0), ("g", 5), ("ZF", 3), ("H", 1), ("AO",), ("g", 6),
+    ("RB",), ("AE",), ("RD",),
 )
 
 
 def kernel(
     x_in, c_in, up_in, down_in, g_in,
     out_hbm, dtok_hbm, gu_hbm, gd_hbm, gg_ref,
-    xo, co, ws, w_in, wz, out_ref, dtok_ref, go, xt, nc, w, relay, gr, gcol, inv_s, pre_s, dh_s, slope, hd, md_s, gs, g, xr, zs, zr,
+    xo, co, ws, w_in, wz, out_ref, dtok_ref, go, xt, nc, w, relay, gr, gcol, inv_s, pre_s, dh_s, slope, hd, md_s, gs, g, xr, zr,
     br, dn, b0, b1, bq0, bq1, d0, d1, dq0, dq1, stage, ga, ggp, ggr, ggx, ggy, ggz, ggc,
     send_sem, recv_sem, copy_sem,
 ):
@@ -441,8 +441,8 @@
         if (s - 1, p, j) in zmsg:
             zmsg[s - 1, p, j].wait_recv()
             val = val + zr[p, s - 1, q].astype(F32)
-        zs[p, s, q] = val.astype(BF16)
-        zmsg[s, p, j] = msg.start(zs.at[p, s, q], zr.at[p, s, q], dev("z", 1 - 2 * p))
+        wz[4 * p + s, q] = val.astype(BF16)
+        zmsg[s, p, j] = msg.start(wz.at[4 * p + s, q], zr.at[p, s, q], dev("z", 1 - 2 * p))
 
     back, hands = {}, {}
 
@@ -647,7 +647,6 @@
             vm((NZ, NY, RP, FM), F32),
             vm((NZ, DZ, FP)),
             vm((2, 4, NY, RP, FM)),
-            vm((2, 4, NY, RP, FM)),
             vm((NX, NY, DX, TB)),
             vm((NX, NY, DE, TB)),
             vm((4, 2, 400, TB)),

time: 108 us -> 105 us (0.972)
  Pallas kernels: 107 us -> 104 us
    pallas_call x1, Pallas kernels: 104 us -> 102 us  [block(): pl.pallas_call(kernel, out_shape=(jax.ShapeDtypeStruct((DX, TB), BF16), j...]
where the time goes in v6:
time: 105 us
  Pallas kernels  104 us (99%)
    pallas_call x1, Pallas kernels, block(): pl.pallas_call(kernel, out_shape=(jax.ShapeDtypeStruct((DX, TB), BF16), j...  102 us
    pallas_call x1, Pallas kernels, on_device(): pl.pallas_call(finish, out_shape=(jax.ShapeDtypeStruct((DX, TB), BF16), j...  2.49 us

profile of v6, /device:TPU:1, one launch (start us, length us, event | category | flops | bytes accessed | tf_op | source)
XLA Modules:
  0.0 104.6 jit_solution(17906610434143993614)
XLA Ops:
  0.6 101.5 %shard_map.92 = (bf16[800,128]{1,0:T(8,128)(2,1)}, bf16[800,128]{1,0:T(8,128)(2,1)}, bf16[100,1600]{1,0:T(8,128)(2,1)}, bf16[100,1600]{1,0:T(8,128)(2,1)}, f32[1,800]{1,0:T(1,128)}) custom-call(bf16[800,128]{1,0:T(8,128)(2,1)} %bitcast.7, bf16[800,128]{1,0:T(8,128)(2,1)} %bitcast.8, bf16[100,1600]{1,0:T(8,128)(2,1)} %up_in.1, bf16[100,1600]{1,0:T(8,128)(2,1)} %bitcast.6, ...), custom_call_target="tpu_custom_call" | custom-call | tf_op jit(solution)/shard_map/pallas_call | solution.py:614
  102.1 2.5 %shard_map.93 = (bf16[800,128]{1,0:T(8,128)(2,1)}, bf16[800,128]{1,0:T(8,128)(2,1)}, f32[100,1600]{1,0:T(8,128)}, f32[100,1600]{1,0:T(8,128)}, f32[800]{0:T(1024)}) custom-call(bf16[800,128]{1,0:T(8,128)(2,1)} %get-tuple-element.15.out_in, bf16[800,128]{1,0:T(8,128)(2,1)} %get-tuple-element.16.dtok_in, bf16[100,1600]{1,0:T(8,128)(2,1)} %get-tuple-element.17.gu_in, ...), custom_call_target="tpu_custom_call" | custom-call | tf_op jit(solution)/shard_map/pallas_call | solution.py:689
